TPU v7x, 512 devices: a whole 4x4x16 slice. The times are simulated.
512 devices in a mesh: seq: 64 (over z, y_lo, core), chan: 8 (over y_hi, x).
Axes of the slice: x: 4, y: 4 (y_hi: 2, y_lo: 2; y = y_hi * 2 + y_lo), z: 16, core: 2. Of those that a mesh axis runs over, the one named last changes fastest.
Arguments:
- query: bfloat16 [8192, 3072], P('seq', 'chan'), may hold values from -6 to 6
- key_in: bfloat16 [8192, 3072], P('seq', 'chan'), may hold values from -6 to 6
- value: bfloat16 [8192, 3072], P('seq', 'chan'), may hold values from -6 to 6
- cotangent: bfloat16 [8192, 3072], P('seq', 'chan'), may hold values from -6 to 6
- filter_raw: bfloat16 [8192, 128], P('seq'), may hold values from -6 to 6
Outputs:
- grad_query: bfloat16 [8192, 3072], P('seq', 'chan')
- grad_key: bfloat16 [8192, 3072], P('seq', 'chan')
- grad_value: bfloat16 [8192, 3072], P('seq', 'chan')
- grad_filter: float32 [8192, 128], P(('seq', 'chan'))
All inputs are finite; a program needn't handle non-finite values.
Results may differ from a plain program's by a relative error of at most 0.012.
Values may be sent and summed in bfloat16 or wider, within the bound.
No kernel may reach another device: no remote copies, remote signals or barrier semaphores. Data moves between devices by JAX's collectives and lax.ppermute only.
A program may use at most 64 MiB of HBM per device.

v0:
```python
import math

import jax
import jax.numpy as jnp
from jax import lax
from jax.sharding import PartitionSpec as P

HIGH = lax.Precision.HIGHEST


def angle_table(rows, cols, modulus):
    left = lax.iota(jnp.int32, rows)[:, None]
    right = lax.iota(jnp.int32, cols)[None, :]
    product = left * right % modulus
    angles = product.astype(jnp.float32) * (2.0 * math.pi / modulus)
    return (jnp.cos(angles), -jnp.sin(angles))


def make_tables(length):
    full_len = 2 * length
    best = 1
    for divisor in range(1, math.isqrt(full_len) + 1):
        if length % divisor == 0:
            best = divisor
    q_len = full_len // best
    cos_q, sin_q = angle_table(q_len, q_len, q_len)
    cos_p, sin_p = angle_table(best, best, best)
    tw_re, tw_im = angle_table(q_len, best, full_len)
    return (q_len, best, (cos_q, sin_q, cos_p, sin_p, tw_re, tw_im))


def forward_dft(signal, setup):
    q_len, p_len, tables = setup
    cos_q, sin_q, cos_p, sin_p, tw_re, tw_im = tables
    half_q = q_len // 2
    rows = signal.reshape(signal.shape[:-1] + (half_q, p_len))
    a_re = jnp.einsum("kn,...np->...kp", cos_q[:, :half_q], rows, precision=HIGH)
    a_im = jnp.einsum("kn,...np->...kp", sin_q[:, :half_q], rows, precision=HIGH)
    b_re = a_re * tw_re - a_im * tw_im
    b_im = a_re * tw_im + a_im * tw_re
    out_re = jnp.einsum("...kn,nm->...km", b_re, cos_p, precision=HIGH) - jnp.einsum(
        "...kn,nm->...km", b_im, sin_p, precision=HIGH
    )
    out_im = jnp.einsum("...kn,nm->...km", b_re, sin_p, precision=HIGH) + jnp.einsum(
        "...kn,nm->...km", b_im, cos_p, precision=HIGH
    )
    return (out_re, out_im)


def inverse_dft(spec_re, spec_im, setup):
    q_len, p_len, tables = setup
    cos_q, sin_q, cos_p, sin_p, tw_re, tw_im = tables
    half_q = q_len // 2
    c_re = jnp.einsum("...kn,nm->...km", spec_re, cos_p, precision=HIGH) + jnp.einsum(
        "...kn,nm->...km", spec_im, sin_p, precision=HIGH
    )
    c_im = jnp.einsum("...kn,nm->...km", spec_im, cos_p, precision=HIGH) - jnp.einsum(
        "...kn,nm->...km", spec_re, sin_p, precision=HIGH
    )
    d_re = c_re * tw_re + c_im * tw_im
    d_im = c_im * tw_re - c_re * tw_im
    result = jnp.einsum("nk,...kp->...np", cos_q[:half_q], d_re, precision=HIGH) + jnp.einsum(
        "nk,...kp->...np", sin_q[:half_q], d_im, precision=HIGH
    )
    return result.reshape(result.shape[:-2] + (half_q * p_len,)) * (1.0 / (q_len * p_len))


def spectral_core(mixed, gated, raw_rows):
    length = mixed.shape[-1]
    setup = make_tables(length)
    filt = raw_rows.astype(jnp.float32) * (1.0 / math.sqrt(length))
    f_re, f_im = forward_dft(filt, setup)
    m_re, m_im = forward_dft(mixed.astype(jnp.float32), setup)
    g_re, g_im = forward_dft(gated.astype(jnp.float32), setup)
    conv = inverse_dft(m_re * f_re - m_im * f_im, m_re * f_im + m_im * f_re, setup).astype(
        jnp.bfloat16
    )
    back_conv = inverse_dft(g_re * f_re + g_im * f_im, g_im * f_re - g_re * f_im, setup).astype(
        jnp.bfloat16
    )
    cross_re = jnp.sum(g_re * m_re + g_im * m_im, axis=0)
    cross_im = jnp.sum(g_im * m_re - g_re * m_im, axis=0)
    filt_grad = inverse_dft(cross_re, cross_im, setup) * (1.0 / math.sqrt(length))
    return (conv, back_conv, filt_grad)


def to_rows(array):
    length, repeat, single, items = array.shape
    return jnp.transpose(array.reshape(length, repeat, items), (1, 2, 0))


def to_cols(array):
    repeat, items, length = array.shape
    return jnp.transpose(array, (2, 0, 1)).reshape(length, repeat, 1, items)


def times_bf16(left, right):
    return (left.astype(jnp.float32) * right.astype(jnp.float32)).astype(jnp.bfloat16)


def local(query, key_in, value, cotangent, filter_raw):
    tok_rows, channels = query.shape
    groups = lax.axis_size("seq")
    filters = filter_raw.shape[1]
    repeat = channels // filters
    per_dev = filters // groups
    raw_four = filter_raw.reshape(tok_rows, 1, groups, per_dev)

    def spread(array):
        return array.reshape(tok_rows, repeat, groups, per_dev)

    q_part = lax.all_to_all(spread(query), "seq", split_axis=2, concat_axis=0, tiled=True)
    k_part = lax.all_to_all(spread(key_in), "seq", split_axis=2, concat_axis=0, tiled=True)
    v_part = lax.all_to_all(spread(value), "seq", split_axis=2, concat_axis=0, tiled=True)
    g_part = lax.all_to_all(spread(cotangent), "seq", split_axis=2, concat_axis=0, tiled=True)
    raw_part = lax.all_to_all(raw_four, "seq", split_axis=2, concat_axis=0, tiled=True)
    q_rows = to_rows(q_part)
    k_rows = to_rows(k_part)
    v_rows = to_rows(v_part)
    g_rows = to_rows(g_part)
    mixed = times_bf16(k_rows, v_rows)
    gated = times_bf16(g_rows, q_rows)
    conv, back_conv, filt_grad = spectral_core(mixed, gated, to_rows(raw_part)[0])
    grad_q = times_bf16(g_rows, conv)
    grad_k = times_bf16(back_conv, v_rows)
    grad_v = times_bf16(back_conv, k_rows)
    grad_q, grad_k, grad_v, filt_part = (
        lax.all_to_all(to_cols(grad_q), "seq", split_axis=0, concat_axis=2, tiled=True),
        lax.all_to_all(to_cols(grad_k), "seq", split_axis=0, concat_axis=2, tiled=True),
        lax.all_to_all(to_cols(grad_v), "seq", split_axis=0, concat_axis=2, tiled=True),
        to_cols(filt_grad[None]),
    )
    grad_query = grad_q.reshape(tok_rows, channels)
    grad_key = grad_k.reshape(tok_rows, channels)
    grad_value = grad_v.reshape(tok_rows, channels)
    at_home = lax.all_to_all(filt_part, "seq", split_axis=0, concat_axis=2, tiled=True).reshape(
        tok_rows, filters
    )
    grad_filter = lax.psum_scatter(at_home, "chan", scatter_dimension=0, tiled=True)
    return (grad_query, grad_key, grad_value, grad_filter)


def solution(mesh):
    placed = (
        P("seq", "chan"),
        P("seq", "chan"),
        P("seq", "chan"),
        P("seq", "chan"),
        P("seq", None),
    )
    return jax.shard_map(
        local,
        mesh=mesh,
        in_specs=placed,
        out_specs=(P("seq", "chan"), P("seq", "chan"), P("seq", "chan"), P(("seq", "chan"), None)),
        check_vma=False,
    )
```

profile of v0, /device:TPU:6, one launch (start us, length us, event | category | flops | bytes accessed | tf_op | source)
XLA Modules:
  0.0 380.5 jit_solution(2649086026096921102)
XLA Ops:
  7.2 1.5 copy.334
  8.6 17.1 %all-to-all-start.3 = ((bf16[128,1,64,2]{0,3,1,2:T(2,128)(2,1)}), bf16[128,1,64,2]{0,3,1,2:T(2,128)(2,1)S(1)}, u32[]{:S(2)}, u32[]{:S(2)}) async-start(bf16[128,1,64,2]{0,3,1,2:T(2,128)(2,1)} %bitcast.21), calls=%async_computation.3 | async-start | bytes 65536 | tf_op jit(solution)/shard_map/all_to_all | solution.py:116
  26.3 1.0 copy.362
  28.0 1.0 copy.324
  29.7 1.0 copy.327
  31.4 1.0 copy.321
  33.4 5.6 %all-to-all-done.3 = bf16[128,1,64,2]{0,3,1,2:T(2,128)(2,1)S(1)} async-done(((bf16[128,1,64,2]{0,3,1,2:T(2,128)(2,1)}), bf16[128,1,64,2]{0,3,1,2:T(2,128)(2,1)S(1)}, u32[]{:S(2)}, u32[]{:S(2)}) %all-to-all-start.3) | async-done | bytes 32800 | tf_op jit(solution)/shard_map/all_to_all | solution.py:116
  39.0 8.0 %all-to-all-start.5 = ((bf16[128,3,64,2]{0,3,1,2:T(2,128)(2,1)}), bf16[128,3,64,2]{0,3,1,2:T(2,128)(2,1)S(1)}, u32[]{:S(2)}, u32[]{:S(2)}) async-start(bf16[128,3,64,2]{0,3,1,2:T(2,128)(2,1)} %copy.363), calls=%async_computation.5 | async-start | bytes 196608 | tf_op jit(solution)/shard_map/all_to_all | solution.py:112
  49.6 13.1 %all-to-all-done.5 = bf16[128,3,64,2]{0,3,1,2:T(2,128)(2,1)S(1)} async-done(((bf16[128,3,64,2]{0,3,1,2:T(2,128)(2,1)}), bf16[128,3,64,2]{0,3,1,2:T(2,128)(2,1)S(1)}, u32[]{:S(2)}, u32[]{:S(2)}) %all-to-all-start.5) | async-done | bytes 98336 | tf_op jit(solution)/shard_map/all_to_all | solution.py:112
  62.7 4.6 %all-to-all-start = ((bf16[128,3,64,2]{0,3,1,2:T(2,128)(2,1)}), bf16[128,3,64,2]{0,3,1,2:T(2,128)(2,1)S(1)}, u32[]{:S(2)}, u32[]{:S(2)}) async-start(bf16[128,3,64,2]{0,3,1,2:T(2,128)(2,1)} %copy.322), calls=%async_computation | async-start | bytes 196608 | tf_op jit(solution)/shard_map/all_to_all | solution.py:115
  68.2 14.9 %all-to-all-done = bf16[128,3,64,2]{0,3,1,2:T(2,128)(2,1)S(1)} async-done(((bf16[128,3,64,2]{0,3,1,2:T(2,128)(2,1)}), bf16[128,3,64,2]{0,3,1,2:T(2,128)(2,1)S(1)}, u32[]{:S(2)}, u32[]{:S(2)}) %all-to-all-start) | async-done | bytes 98336 | tf_op jit(solution)/shard_map/all_to_all | solution.py:115
  83.1 4.8 %all-to-all-start.1 = ((bf16[128,3,64,2]{0,3,1,2:T(2,128)(2,1)}), bf16[128,3,64,2]{0,3,1,2:T(2,128)(2,1)S(1)}, u32[]{:S(2)}, u32[]{:S(2)}) async-start(bf16[128,3,64,2]{0,3,1,2:T(2,128)(2,1)} %copy.325), calls=%async_computation.1 | async-start | bytes 196608 | tf_op jit(solution)/shard_map/all_to_all | solution.py:113
  89.1 1.0 fusion.73
  90.1 1.0 fusion.86
  91.1 1.0 convolution_add_fusion.1
  92.1 1.0 convolution_subtract_fusion.1
  93.9 9.8 %all-to-all-done.1 = bf16[128,3,64,2]{0,3,1,2:T(2,128)(2,1)S(1)} async-done(((bf16[128,3,64,2]{0,3,1,2:T(2,128)(2,1)}), bf16[128,3,64,2]{0,3,1,2:T(2,128)(2,1)S(1)}, u32[]{:S(2)}, u32[]{:S(2)}) %all-to-all-start.1) | async-done | bytes 98336 | tf_op jit(solution)/shard_map/all_to_all | solution.py:113
  103.7 4.8 %all-to-all-start.2 = ((bf16[128,3,64,2]{0,3,1,2:T(2,128)(2,1)}), bf16[128,3,64,2]{0,3,1,2:T(2,128)(2,1)S(1)}, u32[]{:S(2)}, u32[]{:S(2)}) async-start(bf16[128,3,64,2]{0,3,1,2:T(2,128)(2,1)} %copy.328), calls=%async_computation.2 | async-start | bytes 196608 | tf_op jit(solution)/shard_map/all_to_all | solution.py:114
  109.5 14.5 %all-to-all-done.2 = bf16[128,3,64,2]{0,3,1,2:T(2,128)(2,1)S(1)} async-done(((bf16[128,3,64,2]{0,3,1,2:T(2,128)(2,1)}), bf16[128,3,64,2]{0,3,1,2:T(2,128)(2,1)S(1)}, u32[]{:S(2)}, u32[]{:S(2)}) %all-to-all-start.2) | async-done | bytes 98336 | tf_op jit(solution)/shard_map/all_to_all | solution.py:114
  128.2 1.0 fusion.78
  129.2 1.0 fusion.93
  130.2 1.0 convolution_subtract_fusion.3
  131.2 1.0 add_reduce_fusion
  135.4 0.9 convolution_subtract_fusion.4
  139.8 2.6 copy.499
  142.9 38.4 %reduce = f32[8192,2]{1,0:T(8,128)} reduce(f32[8192,1,1,2]{3,2,1,0:T(1,128)} %bitcast.267, f32[]{:T(128)} %broadcast.323), dimensions={1,2}, to_apply=%bitcast.86.reduce_sub_computation | reduce | bytes 131076 | tf_op jit(solution)/shard_map/reshape | solution.py:94
  181.3 5.1 %reshape.262 = f32[64,1,256]{2,1,0:T(1,128)} reshape(f32[8192,2]{1,0:T(8,128)} %reduce) | data formatting | bytes 131072
  186.5 4.6 %all-to-all-start.8 = ((f32[64,1,256]{2,1,0:T(1,128)}), f32[64,1,256]{2,1,0:T(1,128)S(1)}, u32[]{:S(2)}, u32[]{:S(2)}) async-start(f32[64,1,256]{2,1,0:T(1,128)} %reshape.262), calls=%async_computation.8 | async-start | bytes 131072 | tf_op jit(solution)/shard_map/all_to_all | solution.py:136
  191.2 6.9 %copy.360 = bf16[8192,3,1,2]{1,3,2,0:T(2,128)(2,1)} copy(bf16[8192,3,1,2]{0,3,1,2:T(2,128)(2,1)S(1)} %fusion.44) | data formatting | bytes 196608 | tf_op jit(solution)/shard_map/reshape | solution.py:94
  198.1 7.5 %reshape.256 = bf16[64,2,384]{2,1,0:T(2,128)(2,1)} reshape(bf16[8192,1,2,3]{3,2,1,0:T(2,128)(2,1)} %bitcast.268) | data formatting | bytes 196608
  205.5 13.8 %all-to-all-start.4 = ((bf16[64,2,384]{2,1,0:T(2,128)(2,1)}), bf16[64,2,384]{2,1,0:T(2,128)(2,1)S(1)}, u32[]{:S(2)}, u32[]{:S(2)}) async-start(bf16[64,2,384]{2,1,0:T(2,128)(2,1)} %reshape.256), calls=%async_computation.4 | async-start | bytes 196608 | tf_op jit(solution)/shard_map/all_to_all | solution.py:128
  219.3 6.9 %copy.387 = bf16[8192,3,1,2]{1,3,2,0:T(2,128)(2,1)} copy(bf16[8192,3,1,2]{0,3,1,2:T(2,128)(2,1)S(1)} %get-tuple-element.22) | data formatting | bytes 196608 | tf_op jit(solution)/shard_map/reshape | solution.py:94
  226.2 7.5 %reshape.260 = bf16[64,2,384]{2,1,0:T(2,128)(2,1)} reshape(bf16[8192,1,2,3]{3,2,1,0:T(2,128)(2,1)} %bitcast.269) | data formatting | bytes 196608
  233.6 1.4 all-to-all-done.4
  235.0 12.2 %all-to-all-start.7 = ((bf16[64,2,384]{2,1,0:T(2,128)(2,1)}), bf16[64,2,384]{2,1,0:T(2,128)(2,1)S(1)}, u32[]{:S(2)}, u32[]{:S(2)}) async-start(bf16[64,2,384]{2,1,0:T(2,128)(2,1)} %reshape.260), calls=%async_computation.7 | async-start | bytes 196608 | tf_op jit(solution)/shard_map/all_to_all | solution.py:130
  247.2 6.9 %copy.385 = bf16[8192,3,1,2]{1,3,2,0:T(2,128)(2,1)} copy(bf16[8192,3,1,2]{0,3,1,2:T(2,128)(2,1)S(1)} %get-tuple-element.24) | data formatting | bytes 196608 | tf_op jit(solution)/shard_map/reshape | solution.py:94
  254.1 7.5 %reshape.258 = bf16[64,2,384]{2,1,0:T(2,128)(2,1)} reshape(bf16[8192,1,2,3]{3,2,1,0:T(2,128)(2,1)} %bitcast.270) | data formatting | bytes 196608
  261.5 1.4 all-to-all-done.7
  262.9 12.2 %all-to-all-start.6 = ((bf16[64,2,384]{2,1,0:T(2,128)(2,1)}), bf16[64,2,384]{2,1,0:T(2,128)(2,1)S(1)}, u32[]{:S(2)}, u32[]{:S(2)}) async-start(bf16[64,2,384]{2,1,0:T(2,128)(2,1)} %reshape.258), calls=%async_computation.6 | async-start | bytes 196608 | tf_op jit(solution)/shard_map/all_to_all | solution.py:129
  276.2 8.1 %reshape.263 = f32[8192,1,1,2]{3,2,1,0:T(1,128)} reshape(f32[64,256]{1,0:T(8,128)S(1)} %reduce.1) | data formatting | bytes 131072
  284.3 2.8 copy.402
  287.9 9.8 %reshape.257 = bf16[8192,1,2,3]{3,2,1,0:T(2,128)(2,1)} reshape(bf16[64,2,384]{2,1,0:T(2,128)(2,1)S(1)} %all-to-all-done.4) | data formatting | bytes 196608
  297.7 8.6 %copy.361 = bf16[64,128,3,1,2]{1,4,0,2,3:T(2,128)(2,1)S(1)} copy(bf16[64,128,3,1,2]{2,4,1,0,3:T(2,128)(2,1)} %bitcast.272) | data formatting | bytes 196608 | tf_op jit(solution)/shard_map/all_to_all | solution.py:128
  307.1 9.8 %reshape.261 = bf16[8192,1,2,3]{3,2,1,0:T(2,128)(2,1)} reshape(bf16[64,2,384]{2,1,0:T(2,128)(2,1)S(1)} %all-to-all-done.7) | data formatting | bytes 196608
  316.8 8.6 %copy.388 = bf16[64,128,3,1,2]{1,4,0,2,3:T(2,128)(2,1)S(1)} copy(bf16[64,128,3,1,2]{2,4,1,0,3:T(2,128)(2,1)} %bitcast.273) | data formatting | bytes 196608 | tf_op jit(solution)/shard_map/all_to_all | solution.py:130
  326.2 9.8 %reshape.259 = bf16[8192,1,2,3]{3,2,1,0:T(2,128)(2,1)} reshape(bf16[64,2,384]{2,1,0:T(2,128)(2,1)S(1)} %all-to-all-done.6) | data formatting | bytes 196608
  336.0 8.6 %copy.386 = bf16[64,128,3,1,2]{1,4,0,2,3:T(2,128)(2,1)S(1)} copy(bf16[64,128,3,1,2]{2,4,1,0,3:T(2,128)(2,1)} %bitcast.274) | data formatting | bytes 196608 | tf_op jit(solution)/shard_map/all_to_all | solution.py:129
  345.4 28.0 %reduce-scatter.4.cloned.1.call-done = f32[16,128]{1,0:T(8,128)} async-done(((f32[128,128]{1,0:T(8,128)}), f32[16,128]{1,0:T(8,128)}) %reduce-scatter.4.cloned.1.call-update) | async-done | bytes 8208
  (64 shorter events, 25.4 us)
Async XLA Ops:
  8.6 30.4 %all-to-all-start.3 = ((bf16[128,1,64,2]{0,3,1,2:T(2,128)(2,1)}), bf16[128,1,64,2]{0,3,1,2:T(2,128)(2,1)S(1)}, u32[]{:S(2)}, u32[]{:S(2)}) async-start(bf16[128,1,64,2]{0,3,1,2:T(2,128)(2,1)} %bitcast.21), calls=%async_computation.3 | async-start | bytes 65536 | tf_op jit(solution)/shard_map/all_to_all | solution.py:116
  39.0 23.7 %all-to-all-start.5 = ((bf16[128,3,64,2]{0,3,1,2:T(2,128)(2,1)}), bf16[128,3,64,2]{0,3,1,2:T(2,128)(2,1)S(1)}, u32[]{:S(2)}, u32[]{:S(2)}) async-start(bf16[128,3,64,2]{0,3,1,2:T(2,128)(2,1)} %copy.363), calls=%async_computation.5 | async-start | bytes 196608 | tf_op jit(solution)/shard_map/all_to_all | solution.py:112
  62.7 20.3 %all-to-all-start = ((bf16[128,3,64,2]{0,3,1,2:T(2,128)(2,1)}), bf16[128,3,64,2]{0,3,1,2:T(2,128)(2,1)S(1)}, u32[]{:S(2)}, u32[]{:S(2)}) async-start(bf16[128,3,64,2]{0,3,1,2:T(2,128)(2,1)} %copy.322), calls=%async_computation | async-start | bytes 196608 | tf_op jit(solution)/shard_map/all_to_all | solution.py:115
  83.1 20.6 %all-to-all-start.1 = ((bf16[128,3,64,2]{0,3,1,2:T(2,128)(2,1)}), bf16[128,3,64,2]{0,3,1,2:T(2,128)(2,1)S(1)}, u32[]{:S(2)}, u32[]{:S(2)}) async-start(bf16[128,3,64,2]{0,3,1,2:T(2,128)(2,1)} %copy.325), calls=%async_computation.1 | async-start | bytes 196608 | tf_op jit(solution)/shard_map/all_to_all | solution.py:113
  103.7 20.3 %all-to-all-start.2 = ((bf16[128,3,64,2]{0,3,1,2:T(2,128)(2,1)}), bf16[128,3,64,2]{0,3,1,2:T(2,128)(2,1)S(1)}, u32[]{:S(2)}, u32[]{:S(2)}) async-start(bf16[128,3,64,2]{0,3,1,2:T(2,128)(2,1)} %copy.328), calls=%async_computation.2 | async-start | bytes 196608 | tf_op jit(solution)/shard_map/all_to_all | solution.py:114
  186.5 19.1 %all-to-all-start.8 = ((f32[64,1,256]{2,1,0:T(1,128)}), f32[64,1,256]{2,1,0:T(1,128)S(1)}, u32[]{:S(2)}, u32[]{:S(2)}) async-start(f32[64,1,256]{2,1,0:T(1,128)} %reshape.262), calls=%async_computation.8 | async-start | bytes 131072 | tf_op jit(solution)/shard_map/all_to_all | solution.py:136
  205.5 29.5 %all-to-all-start.4 = ((bf16[64,2,384]{2,1,0:T(2,128)(2,1)}), bf16[64,2,384]{2,1,0:T(2,128)(2,1)S(1)}, u32[]{:S(2)}, u32[]{:S(2)}) async-start(bf16[64,2,384]{2,1,0:T(2,128)(2,1)} %reshape.256), calls=%async_computation.4 | async-start | bytes 196608 | tf_op jit(solution)/shard_map/all_to_all | solution.py:128
  235.0 27.9 %all-to-all-start.7 = ((bf16[64,2,384]{2,1,0:T(2,128)(2,1)}), bf16[64,2,384]{2,1,0:T(2,128)(2,1)S(1)}, u32[]{:S(2)}, u32[]{:S(2)}) async-start(bf16[64,2,384]{2,1,0:T(2,128)(2,1)} %reshape.260), calls=%async_computation.7 | async-start | bytes 196608 | tf_op jit(solution)/shard_map/all_to_all | solution.py:130
  262.9 63.3 %all-to-all-start.6 = ((bf16[64,2,384]{2,1,0:T(2,128)(2,1)}), bf16[64,2,384]{2,1,0:T(2,128)(2,1)S(1)}, u32[]{:S(2)}, u32[]{:S(2)}) async-start(bf16[64,2,384]{2,1,0:T(2,128)(2,1)} %reshape.258), calls=%async_computation.6 | async-start | bytes 196608 | tf_op jit(solution)/shard_map/all_to_all | solution.py:129
  275.1 98.3 %reduce-scatter.4.cloned.1.call-start = ((), (), s32[]{:S(2)}) async-start(), calls=%async_computation.10 | async-start | bytes 73728
Sparse Core Ops, SparseCore 0:
  288.0 85.3 reduce-scatter.3
where the time goes:
time: 388 us; the launch traced here: 380 us
  local copies, waits for them, and re-layouts  130 us (34%)
  waiting for transfers between devices  88.7 us (23%)
  starting transfers between devices  82.4 us (21%)
  other arithmetic  40.8 us (11%)
  matrix products  24.3 us (6%)
  between operations  14.8 us (4%)
    unnamed x17, local copies, waits for them, and re-layouts  73.4 us
    reshape x3, other arithmetic, to_cols(): return jnp.transpose(array, (2, 0, 1)).reshape(length, repeat, 1, items)  38.7 us
    unnamed x2, waiting for transfers between devices  28.1 us
    reshape x4, local copies, waits for them, and re-layouts, to_cols(): return jnp.transpose(array, (2, 0, 1)).reshape(length, repeat, 1, items)  21.1 us
    all_to_all x1, starting transfers between devices, local(): lax.all_to_all(raw_four, 'seq', split_axis=2, concat_axis=0, tiled=True)  17.1 us
    all_to_all x1, waiting for transfers between devices, local(): lax.all_to_all(spread(cotangent), 'seq', split_axis=2, concat_axis=0, til...  14.9 us
    all_to_all x1, waiting for transfers between devices, local(): lax.all_to_all(spread(value), 'seq', split_axis=2, concat_axis=0, tiled=T...  14.5 us
    all_to_all x1, starting transfers between devices, local(): lax.all_to_all(to_cols(grad_q), 'seq', split_axis=0, concat_axis=2, tiled...  13.8 us
  transfers between devices with their start and end apart: 10, of which 8 were waited for; matrix products, arithmetic and copies ran while one was open for 34% of the time, Pallas kernels for 0%

commit v1 on v0

v1 whole, which is shorter than its diff:
```python
import math

import numpy as np
import jax
import jax.numpy as jnp
from jax import lax
from jax.experimental import pallas as pl
from jax.experimental.pallas import tpu as pltpu
from jax.sharding import PartitionSpec as P

F32 = jnp.float32
BF16 = jnp.bfloat16
VMEM_LIMIT = 48 * 1024 * 1024


def split_table(table):
    high = table.astype(BF16)
    low = (table - high.astype(np.float64)).astype(BF16)
    return high, low


def make_tables(blocks, width):
    length = blocks * width
    j = np.arange(blocks)
    k1 = np.arange(blocks) + 0.25
    r = np.arange(width)
    k2 = np.arange(width)
    angle_a = 2.0 * np.pi * np.outer(k1, j) / blocks
    outer_t = np.concatenate([np.cos(angle_a), -np.sin(angle_a)], 0)
    angle_t = 2.0 * np.pi * np.outer(k1, r) / length
    twist = np.concatenate([np.cos(angle_t), -np.sin(angle_t)], 1).astype(np.float32)
    angle_b = 2.0 * np.pi * np.outer(r, k2) / width
    cos_b, sin_b = np.cos(angle_b), np.sin(angle_b)
    inner_t = np.block([[cos_b, -sin_b], [sin_b, cos_b]])
    a_hi, a_lo = split_table(outer_t)
    b_hi, b_lo = split_table(inner_t)
    fwd_a = np.concatenate([a_hi, a_lo], 1)
    fwd_b = np.concatenate([b_hi, b_hi, b_lo], 0)
    inv_b = np.concatenate([b_hi.T, b_hi.T, b_lo.T], 0)
    inv_a = np.concatenate([a_hi.T, a_hi.T, a_lo.T], 1)
    return fwd_a, twist, fwd_b, inv_b, inv_a


def split(value):
    high = value.astype(BF16)
    low = (value - high.astype(F32)).astype(BF16)
    return high, low


def mul(left, right):
    return jnp.dot(left, right, preferred_element_type=F32)


def to_spectra(cols, fwd_a, twist, fwd_b):
    blocks, width = cols[0].shape
    data = jnp.concatenate(cols, 1)
    part = mul(fwd_a, jnp.concatenate([data, data], 0))
    t_re, t_im = twist[:, :width], twist[:, width:]
    rows = []
    for s in range(len(cols)):
        a_re = part[:blocks, s * width : (s + 1) * width]
        a_im = part[blocks:, s * width : (s + 1) * width]
        rows.append(jnp.concatenate([a_re * t_re - a_im * t_im, a_re * t_im + a_im * t_re], 1))
    high, low = split(jnp.concatenate(rows, 0))
    return mul(jnp.concatenate([high, low, high], 1), fwd_b)


def from_spectra(spec, twist, inv_b, inv_a, scale):
    blocks = twist.shape[0]
    width = twist.shape[1] // 2
    count = spec.shape[0] // blocks
    high, low = split(spec)
    part = mul(jnp.concatenate([high, low, high], 1), inv_b)
    t_re, t_im = twist[:, :width], twist[:, width:]
    cols = []
    for s in range(count):
        d_re = part[s * blocks : (s + 1) * blocks, :width]
        d_im = part[s * blocks : (s + 1) * blocks, width:]
        cols.append(jnp.concatenate([d_re * t_re + d_im * t_im, d_im * t_re - d_re * t_im], 0))
    high, low = split(jnp.concatenate(cols, 1))
    return mul(inv_a, jnp.concatenate([high, low, high], 0)) * scale


def gate_kernel(repeat, left_ref, right_ref, *refs):
    out_ref, hold = refs[-2], refs[-1]
    width = left_ref.shape[0]
    per = out_ref.shape[0] // hold.shape[0] * 8
    blocks = out_ref.shape[0] // per
    fils = width // blocks
    prod = left_ref[...].astype(F32) * right_ref[...].astype(F32)
    prod = prod.astype(BF16).astype(F32)
    parts = [prod[:, c * width : (c + 1) * width] for c in range(repeat)]
    if len(refs) == 3:
        parts.append(refs[0][...].astype(F32))
    else:
        parts.append(jnp.zeros((width, width), F32))
    for c, part in enumerate(parts):
        flipped = part.T
        for f in range(fils):
            hold[pl.ds(c * fils + f, blocks, stride=per), :] = flipped[f * blocks : (f + 1) * blocks]
    out_ref[...] = hold[...].astype(BF16)


def gate(left, right, *extra):
    width, channels = left.shape
    rows = 64 * 8
    return pl.pallas_call(
        lambda *refs: gate_kernel(channels // width, *refs),
        out_shape=jax.ShapeDtypeStruct((rows, width), BF16),
        scratch_shapes=[pltpu.VMEM((rows, width), F32)],
        compiler_params=pltpu.CompilerParams(vmem_limit_bytes=VMEM_LIMIT),
        name="gate",
    )(left, right, *extra)


def take_columns(ref, hold, per, blocks):
    hold[...] = ref[...].astype(F32)
    return [hold[pl.ds(s, blocks, stride=per), :].astype(BF16) for s in range(per)]


def times(a, b):
    w = a.shape[1] // 2
    a_re, a_im, b_re, b_im = a[:, :w], a[:, w:], b[:, :w], b[:, w:]
    return jnp.concatenate([a_re * b_re - a_im * b_im, a_re * b_im + a_im * b_re], 1)


def times_conj(a, b):
    w = a.shape[1] // 2
    a_re, a_im, b_re, b_im = a[:, :w], a[:, w:], b[:, :w], b[:, w:]
    return jnp.concatenate([a_re * b_re + a_im * b_im, a_im * b_re - a_re * b_im], 1)


def put_rows(out_ref, hold, result, per, count, blocks, width):
    for s in range(count):
        hold[pl.ds(s, blocks, stride=per), :] = result[:, s * width : (s + 1) * width]
    for s in range(count, per):
        hold[pl.ds(s, blocks, stride=per), :] = jnp.zeros((blocks, width), F32)
    out_ref[...] = hold[...].astype(BF16)


def conv_kernel(repeat, fils, scale, x_ref, fa, tw, fb, ib, ia, out_ref, spec_ref, hold):
    blocks = tw.shape[0]
    width = tw.shape[1] // 2
    per = (repeat + 1) * fils
    count = repeat * fils
    cols = take_columns(x_ref, hold, per, blocks)
    spec = to_spectra(cols, fa[...], tw[...], fb[...])
    spec_ref[...] = spec
    taps = spec[count * blocks :]
    prods = [times(spec[s * fils * blocks : (s + 1) * fils * blocks], taps) for s in range(repeat)]
    result = from_spectra(jnp.concatenate(prods, 0), tw[...], ib[...], ia[...], scale)
    put_rows(out_ref, hold, result, per, count, blocks, width)


def back_kernel(repeat, fils, scale, x_ref, spec_ref, fa, tw, fb, ib, ia, out_ref, hold):
    blocks = tw.shape[0]
    width = tw.shape[1] // 2
    per = (repeat + 1) * fils
    count = repeat * fils
    cols = take_columns(x_ref, hold, per, blocks)[:count]
    spec = to_spectra(cols, fa[...], tw[...], fb[...])
    step = fils * blocks
    taps = spec_ref[count * blocks :]
    prods = []
    cross = None
    for s in range(repeat):
        gated = spec[s * step : (s + 1) * step]
        prods.append(times_conj(gated, taps))
        term = times_conj(gated, spec_ref[s * step : (s + 1) * step])
        cross = term if cross is None else cross + term
    prods.append(cross)
    result = from_spectra(jnp.concatenate(prods, 0), tw[...], ib[...], ia[...], scale)
    put_rows(out_ref, hold, result, per, per, blocks, width)


def back_rows(hold, per, blocks, width, c):
    fils = width // blocks
    rows = [hold[pl.ds(c * fils + f, blocks, stride=per), :] for f in range(fils)]
    return jnp.concatenate(rows, 0).T


def query_kernel(repeat, conv_ref, cot_ref, out_ref, hold):
    width = cot_ref.shape[0]
    per = conv_ref.shape[0] // 64
    hold[...] = conv_ref[...].astype(F32)
    for c in range(repeat):
        at = slice(c * width, (c + 1) * width)
        conv = back_rows(hold, per, 64, width, c)
        out_ref[:, at] = (cot_ref[:, at].astype(F32) * conv).astype(BF16)


def input_kernel(repeat, back_ref, value_ref, key_ref, grad_key, grad_value, taps_ref, hold):
    width = value_ref.shape[0]
    per = back_ref.shape[0] // 64
    hold[...] = back_ref[...].astype(F32)
    taps_ref[...] = back_rows(hold, per, 64, width, repeat).astype(BF16)
    for c in range(repeat):
        at = slice(c * width, (c + 1) * width)
        back = back_rows(hold, per, 64, width, c)
        grad_key[:, at] = (back * value_ref[:, at].astype(F32)).astype(BF16)
        grad_value[:, at] = (back * key_ref[:, at].astype(F32)).astype(BF16)


def sum_kernel(part_ref, out_ref):
    rows = out_ref.shape[0]
    total = part_ref[:rows].astype(F32)
    for c in range(1, part_ref.shape[0] // rows):
        total = total + part_ref[c * rows : (c + 1) * rows].astype(F32)
    out_ref[...] = total


def local(query, key_in, value, cotangent, filter_raw):
    width, channels = query.shape
    blocks = lax.axis_size("seq")
    groups = lax.axis_size("chan")
    length = blocks * width
    filters = filter_raw.shape[1]
    repeat = channels // filters
    fils = filters // blocks
    per = (repeat + 1) * fils
    scale = 1.0 / (length * math.sqrt(length))
    fwd_a, twist, fwd_b, inv_b, inv_a = (jnp.asarray(t) for t in make_tables(blocks, width))
    params = pltpu.CompilerParams(vmem_limit_bytes=VMEM_LIMIT)
    packed = jax.ShapeDtypeStruct((blocks * per, width), BF16)
    hold = pltpu.VMEM((blocks * per, width), F32)

    def swap(array, axis):
        return lax.all_to_all(array, axis, split_axis=0, concat_axis=0, tiled=True)

    mixed = swap(gate(key_in, value, filter_raw), "seq")
    gated = swap(gate(cotangent, query), "seq")
    conv, spec = pl.pallas_call(
        lambda *refs: conv_kernel(repeat, fils, scale, *refs),
        out_shape=(packed, jax.ShapeDtypeStruct((per * blocks, 2 * width), F32)),
        scratch_shapes=[hold],
        compiler_params=params,
        name="conv",
    )(mixed, fwd_a, twist, fwd_b, inv_b, inv_a)
    conv = swap(conv, "seq")
    back = pl.pallas_call(
        lambda *refs: back_kernel(repeat, fils, scale, *refs),
        out_shape=packed,
        scratch_shapes=[hold],
        compiler_params=params,
        name="back",
    )(gated, spec, fwd_a, twist, fwd_b, inv_b, inv_a)
    back = swap(back, "seq")
    like = jax.ShapeDtypeStruct((width, channels), BF16)
    grad_query = pl.pallas_call(
        lambda *refs: query_kernel(repeat, *refs),
        out_shape=like,
        scratch_shapes=[hold],
        compiler_params=params,
        name="grad_query",
    )(conv, cotangent)
    grad_key, grad_value, taps = pl.pallas_call(
        lambda *refs: input_kernel(repeat, *refs),
        out_shape=(like, like, jax.ShapeDtypeStruct((width, filters), BF16)),
        scratch_shapes=[hold],
        compiler_params=params,
        name="grad_inputs",
    )(back, value, key_in)
    taps = swap(taps, "chan")
    grad_filter = pl.pallas_call(
        sum_kernel,
        out_shape=jax.ShapeDtypeStruct((width // groups, filters), F32),
        compiler_params=params,
        name="grad_filter",
    )(taps)
    return (grad_query, grad_key, grad_value, grad_filter)


def solution(mesh):
    placed = (
        P("seq", "chan"),
        P("seq", "chan"),
        P("seq", "chan"),
        P("seq", "chan"),
        P("seq", None),
    )
    return jax.shard_map(
        local,
        mesh=mesh,
        in_specs=placed,
        out_specs=(P("seq", "chan"), P("seq", "chan"), P("seq", "chan"), P(("seq", "chan"), None)),
        check_vma=False,
    )
```

time: 388 us -> 119 us (0.31); the launches traced: 380 us -> 117 us
  local copies, waits for them, and re-layouts: 130 us -> 2.57 us
  starting transfers between devices: 82.4 us -> 33.8 us
  other arithmetic: 40.8 us -> 0 us
  waiting for transfers between devices: 88.7 us -> 52.4 us
  matrix products: 24.3 us -> 0 us
  blocking collectives: 0 us -> 20.8 us
  between operations: 14.8 us -> 0.76 us
  Pallas kernels: 0 us -> 6.98 us
    unnamed x17 -> x24, local copies, waits for them, and re-layouts: 73.4 us -> 2.57 us
    all_to_all x9 -> x4, starting transfers between devices: 82.1 us -> 33.8 us  [swap(): return lax.all_to_all(array, axis, split_axis=0, concat_axis=0, tiled=True)]
    reshape x3 -> x0, other arithmetic: 38.7 us -> none  [to_cols(): return jnp.transpose(array, (2, 0, 1)).reshape(length, repeat, 1, items)]
    all_to_all x4 -> x0, local copies, waits for them, and re-layouts: 28.7 us -> none  [the longest x1 8.61 us: local(): lax.all_to_all(to_cols(grad_v), 'seq', split_axis=0, concat_axis=2, tiled...]
    unnamed x2 -> x0, waiting for transfers between devices: 28.1 us -> none
    dot_general x36 -> x0, matrix products: 24.3 us -> none  [the longest x3 2.55 us: forward_dft(): jnp.einsum('...kn,nm->...km', b_im, sin_p, precision=HIGH)]
    reshape x10 -> x0, local copies, waits for them, and re-layouts: 24.1 us -> none  [the longest x4 21.1 us: to_cols(): return jnp.transpose(array, (2, 0, 1)).reshape(length, repeat, 1, items)]
    all_to_all x0 -> x1, blocking collectives: none -> 20.8 us  [swap(): return lax.all_to_all(array, axis, split_axis=0, concat_axis=0, tiled=True)]
  transfers between devices with their start and end apart: 10 -> 4, of which waited for: 8 -> 4; matrix products, arithmetic and copies ran while one was open for 34% -> 0% of each run, Pallas kernels for 0% -> 4%
where the time goes in v1:
time: 119 us; the launch traced here: 117 us
  waiting for transfers between devices  52.4 us (44%)
  starting transfers between devices  33.8 us (28%)
  blocking collectives  20.8 us (17%)
  Pallas kernels  6.98 us (6%)
  local copies, waits for them, and re-layouts  2.57 us (2%)
    all_to_all x4, waiting for transfers between devices, swap(): return lax.all_to_all(array, axis, split_axis=0, concat_axis=0, tiled=True)  52.4 us
    all_to_all x4, starting transfers between devices, swap(): return lax.all_to_all(array, axis, split_axis=0, concat_axis=0, tiled=True)  33.8 us
    all_to_all x1, blocking collectives, swap(): return lax.all_to_all(array, axis, split_axis=0, concat_axis=0, tiled=True)  20.8 us
    unnamed x24, local copies, waits for them, and re-layouts  2.57 us
  transfers between devices with their start and end apart: 4, of which 4 were waited for; matrix products, arithmetic and copies ran while one was open for 0% of the time, Pallas kernels for 4%

profile of v1, /device:TPU:6, one launch (start us, length us, event | category | flops | bytes accessed | tf_op | source)
XLA Modules:
  0.0 117.3 jit_solution(7661967106565263199)
XLA Ops:
  0.6 0.0 copy-start.2
  0.6 0.9 copy-done.2
  1.5 0.0 copy-start.4
  1.5 0.9 copy-done.4
  2.4 0.0 copy-start.11
  2.4 0.8 copy-done.11
  3.2 0.0 copy-start.6
  3.2 0.0 copy-start.10
  3.2 0.0 copy-start.8
  3.2 0.0 copy-start.9
  3.2 0.8 gate.2
  4.0 0.0 copy-start
  4.0 0.0 copy-start.1
  4.0 17.2 %all-to-all-start = ((bf16[64,8,128]{2,1,0:T(8,128)(2,1)}), bf16[64,8,128]{2,1,0:T(8,128)(2,1)S(1)}, u32[]{:S(2)}, u32[]{:S(2)}) async-start(bf16[64,8,128]{2,1,0:T(8,128)(2,1)} %bitcast), calls=%async_computation | async-start | bytes 262144 | tf_op jit(solution)/shard_map/all_to_all | solution.py:228
  21.2 0.0 copy-done.6
  21.2 0.0 copy-done.10
  21.2 0.8 gate.3
  22.0 16.2 %all-to-all-done = bf16[64,8,128]{2,1,0:T(8,128)(2,1)S(1)} async-done(((bf16[64,8,128]{2,1,0:T(8,128)(2,1)}), bf16[64,8,128]{2,1,0:T(8,128)(2,1)S(1)}, u32[]{:S(2)}, u32[]{:S(2)}) %all-to-all-start) | async-done | bytes 131104 | tf_op jit(solution)/shard_map/all_to_all | solution.py:228
  38.3 0.0 copy-start.7
  38.3 4.7 %all-to-all-start.2 = ((bf16[64,8,128]{2,1,0:T(8,128)(2,1)}), bf16[64,8,128]{2,1,0:T(8,128)(2,1)S(1)}, u32[]{:S(2)}, u32[]{:S(2)}) async-start(bf16[64,8,128]{2,1,0:T(8,128)(2,1)} %bitcast.4), calls=%async_computation.2 | async-start | bytes 262144 | tf_op jit(solution)/shard_map/all_to_all | solution.py:228
  43.0 0.0 copy-done.8
  43.0 0.0 copy-done.9
  43.0 0.0 copy-done
  43.0 0.0 copy-done.1
  43.0 0.0 copy-done.7
  43.1 2.0 %conv.1 = (bf16[512,128]{1,0:T(8,128)(2,1)}, f32[512,256]{1,0:T(8,128)S(1)}) custom-call(bf16[512,128]{1,0:T(8,128)(2,1)S(1)} %bitcast.13, bf16[128,128]{1,0:T(8,128)(2,1)S(1)} %copy-done.9, f32[64,256]{1,0:T(8,128)S(1)} %copy-done.7, bf16[768,256]{1,0:T(8,128)(2,1)S(1)} %copy-done, bf16[768,256]{1,0:T(8,128)(2,1)S(1)} %copy-done.1, ...), custom_call_target="tpu_custom_call" | custom-call | tf_op jit(solution)/shard_map/conv/pallas_call | solution.py:232
  45.0 15.0 %all-to-all-done.2 = bf16[64,8,128]{2,1,0:T(8,128)(2,1)S(1)} async-done(((bf16[64,8,128]{2,1,0:T(8,128)(2,1)}), bf16[64,8,128]{2,1,0:T(8,128)(2,1)S(1)}, u32[]{:S(2)}, u32[]{:S(2)}) %all-to-all-start.2) | async-done | bytes 131104 | tf_op jit(solution)/shard_map/all_to_all | solution.py:228
  60.0 1.3 %back.1 = bf16[512,128]{1,0:T(8,128)(2,1)S(1)} custom-call(bf16[512,128]{1,0:T(8,128)(2,1)S(1)} %bitcast.12, f32[512,256]{1,0:T(8,128)S(1)} %get-tuple-element.10.refs_1_, bf16[128,128]{1,0:T(8,128)(2,1)S(1)} %copy-done.9, f32[64,256]{1,0:T(8,128)S(1)} %copy-done.7, bf16[768,256]{1,0:T(8,128)(2,1)S(1)} %copy-done, bf16[768,256]{1,0:T(8,128)(2,1)S(1)} %copy-done.1, ...), custom_call_target="tpu_custom_call" | custom-call | tf_op jit(solution)/shard_map/back/pallas_call | solution.py:240
  61.3 20.8 %all_to_all.55 = bf16[64,8,128]{2,1,0:T(8,128)(2,1)S(1)} all-to-all(bf16[64,8,128]{2,1,0:T(8,128)(2,1)S(1)} %bitcast.14), channel_id=1, replica_groups=mesh['seq'=64,'chan'=8] {'seq'}, dimensions={0} | all-to-all | bytes 262144 | tf_op jit(solution)/shard_map/all_to_all | solution.py:228
  82.1 0.0 copy-start.3
  82.1 0.0 copy-start.5
  82.1 4.7 %all-to-all-start.1 = ((bf16[64,8,128]{2,1,0:T(8,128)(2,1)}), bf16[64,8,128]{2,1,0:T(8,128)(2,1)S(1)}, u32[]{:S(2)}, u32[]{:S(2)}) async-start(bf16[64,8,128]{2,1,0:T(8,128)(2,1)} %bitcast.2), calls=%async_computation.1 | async-start | bytes 262144 | tf_op jit(solution)/shard_map/all_to_all | solution.py:228
  86.8 0.0 copy-done.3
  86.8 0.0 copy-done.5
  86.8 0.8 grad_inputs.1
  87.7 16.2 %all-to-all-done.1 = bf16[64,8,128]{2,1,0:T(8,128)(2,1)S(1)} async-done(((bf16[64,8,128]{2,1,0:T(8,128)(2,1)}), bf16[64,8,128]{2,1,0:T(8,128)(2,1)S(1)}, u32[]{:S(2)}, u32[]{:S(2)}) %all-to-all-start.1) | async-done | bytes 131104 | tf_op jit(solution)/shard_map/all_to_all | solution.py:228
  103.8 7.1 %all-to-all-start.4 = ((bf16[8,16,128]{2,1,0:T(8,128)(2,1)}), bf16[8,16,128]{2,1,0:T(8,128)(2,1)S(1)}, u32[]{:S(2)}, u32[]{:S(2)}) async-start(bf16[8,16,128]{2,1,0:T(8,128)(2,1)} %bitcast.8), calls=%async_computation.4 | async-start | bytes 65536 | tf_op jit(solution)/shard_map/all_to_all | solution.py:228
  110.9 0.8 grad_query.1
  111.7 5.0 %all-to-all-done.4 = bf16[8,16,128]{2,1,0:T(8,128)(2,1)S(1)} async-done(((bf16[8,16,128]{2,1,0:T(8,128)(2,1)}), bf16[8,16,128]{2,1,0:T(8,128)(2,1)S(1)}, u32[]{:S(2)}, u32[]{:S(2)}) %all-to-all-start.4) | async-done | bytes 32800 | tf_op jit(solution)/shard_map/all_to_all | solution.py:228
  116.7 0.6 grad_filter.1
Async XLA Ops:
  0.6 0.9 copy-start.2
  1.5 0.9 copy-start.4
  2.4 0.8 copy-start.11
  3.2 18.0 %copy-start.6 = (bf16[128,384]{1,0:T(8,128)(2,1)S(1)}, bf16[128,384]{1,0:T(8,128)(2,1)}, u32[]{:S(2)}) copy-start(bf16[128,384]{1,0:T(8,128)(2,1)} %refs_0_.3) | copy-start | bytes 294916
  3.2 18.0 %copy-start.10 = (bf16[128,384]{1,0:T(8,128)(2,1)S(1)}, bf16[128,384]{1,0:T(8,128)(2,1)}, u32[]{:S(2)}) copy-start(bf16[128,384]{1,0:T(8,128)(2,1)} %refs_1_.7) | copy-start | bytes 294916
  3.2 39.8 %copy-start.8 = (bf16[64,384]{1,0:T(8,128)(2,1)S(1)}, bf16[64,384]{1,0:T(8,128)(2,1)}, u32[]{:S(2)}) copy-start(bf16[64,384]{1,0:T(8,128)(2,1)} %constant.14.clone.refs_5_.refs_6_) | copy-start | bytes 147460
  3.2 39.8 %copy-start.9 = (bf16[128,128]{1,0:T(8,128)(2,1)S(1)}, bf16[128,128]{1,0:T(8,128)(2,1)}, u32[]{:S(2)}) copy-start(bf16[128,128]{1,0:T(8,128)(2,1)} %constant.10.clone.refs_1_.refs_2_) | copy-start | bytes 98308
  4.0 39.1 %copy-start = (bf16[768,256]{1,0:T(8,128)(2,1)S(1)}, bf16[768,256]{1,0:T(8,128)(2,1)}, u32[]{:S(2)}) copy-start(bf16[768,256]{1,0:T(8,128)(2,1)} %constant.12.clone.refs_3_.refs_4_) | copy-start | bytes 1179652
  4.0 39.1 %copy-start.1 = (bf16[768,256]{1,0:T(8,128)(2,1)S(1)}, bf16[768,256]{1,0:T(8,128)(2,1)}, u32[]{:S(2)}) copy-start(bf16[768,256]{1,0:T(8,128)(2,1)} %constant.13.clone.refs_4_.refs_5_) | copy-start | bytes 1179652
  4.0 34.3 %all-to-all-start = ((bf16[64,8,128]{2,1,0:T(8,128)(2,1)}), bf16[64,8,128]{2,1,0:T(8,128)(2,1)S(1)}, u32[]{:S(2)}, u32[]{:S(2)}) async-start(bf16[64,8,128]{2,1,0:T(8,128)(2,1)} %bitcast), calls=%async_computation | async-start | bytes 262144 | tf_op jit(solution)/shard_map/all_to_all | solution.py:228
  38.3 4.8 %copy-start.7 = (f32[64,256]{1,0:T(8,128)S(1)}, f32[64,256]{1,0:T(8,128)}, u32[]{:S(2)}) copy-start(f32[64,256]{1,0:T(8,128)} %constant.11.clone.refs_2_.refs_3_) | copy-start | bytes 196612
  38.3 21.8 %all-to-all-start.2 = ((bf16[64,8,128]{2,1,0:T(8,128)(2,1)}), bf16[64,8,128]{2,1,0:T(8,128)(2,1)S(1)}, u32[]{:S(2)}, u32[]{:S(2)}) async-start(bf16[64,8,128]{2,1,0:T(8,128)(2,1)} %bitcast.4), calls=%async_computation.2 | async-start | bytes 262144 | tf_op jit(solution)/shard_map/all_to_all | solution.py:228
  82.1 4.7 %copy-start.3 = (bf16[128,384]{1,0:T(8,128)(2,1)S(1)}, bf16[128,384]{1,0:T(8,128)(2,1)}, u32[]{:S(2)}) copy-start(bf16[128,384]{1,0:T(8,128)(2,1)} %refs_2_.5) | copy-start | bytes 294916
  82.1 4.7 %copy-start.5 = (bf16[128,384]{1,0:T(8,128)(2,1)S(1)}, bf16[128,384]{1,0:T(8,128)(2,1)}, u32[]{:S(2)}) copy-start(bf16[128,384]{1,0:T(8,128)(2,1)} %refs_1_.8) | copy-start | bytes 294916
  82.1 21.7 %all-to-all-start.1 = ((bf16[64,8,128]{2,1,0:T(8,128)(2,1)}), bf16[64,8,128]{2,1,0:T(8,128)(2,1)S(1)}, u32[]{:S(2)}, u32[]{:S(2)}) async-start(bf16[64,8,128]{2,1,0:T(8,128)(2,1)} %bitcast.2), calls=%async_computation.1 | async-start | bytes 262144 | tf_op jit(solution)/shard_map/all_to_all | solution.py:228
  103.8 12.9 %all-to-all-start.4 = ((bf16[8,16,128]{2,1,0:T(8,128)(2,1)}), bf16[8,16,128]{2,1,0:T(8,128)(2,1)S(1)}, u32[]{:S(2)}, u32[]{:S(2)}) async-start(bf16[8,16,128]{2,1,0:T(8,128)(2,1)} %bitcast.8), calls=%async_computation.4 | async-start | bytes 65536 | tf_op jit(solution)/shard_map/all_to_all | solution.py:228

commit v2 on v1

v2 whole, which is shorter than its diff:
```python
import functools
import math

import numpy as np
import jax
import jax.numpy as jnp
from jax import lax
from jax.experimental import pallas as pl
from jax.experimental.pallas import tpu as pltpu
from jax.sharding import PartitionSpec as P

F32 = jnp.float32
BF16 = jnp.bfloat16
VMEM_LIMIT = 48 * 1024 * 1024


def split_table(table):
    high = table.astype(BF16)
    low = (table - high.astype(np.float64)).astype(BF16)
    return high, low


def make_tables(blocks, width):
    length = blocks * width
    j = np.arange(blocks)
    k1 = np.arange(blocks) + 0.25
    r = np.arange(width)
    k2 = np.arange(width)
    angle_a = 2.0 * np.pi * np.outer(k1, j) / blocks
    outer_t = np.concatenate([np.cos(angle_a), -np.sin(angle_a)], 0)
    angle_t = 2.0 * np.pi * np.outer(k1, r) / length
    twist = np.concatenate([np.cos(angle_t), -np.sin(angle_t)], 1).astype(np.float32)
    angle_b = 2.0 * np.pi * np.outer(r, k2) / width
    cos_b, sin_b = np.cos(angle_b), np.sin(angle_b)
    inner_t = np.block([[cos_b, -sin_b], [sin_b, cos_b]])
    a_hi, a_lo = split_table(outer_t)
    b_hi, b_lo = split_table(inner_t)
    fwd_a = np.concatenate([a_hi, a_lo], 1)
    fwd_b = np.concatenate([b_hi, b_hi, b_lo], 0)
    inv_b = np.concatenate([b_hi.T, b_hi.T, b_lo.T], 0)
    inv_a = np.concatenate([a_hi.T, a_hi.T, a_lo.T], 1)
    return fwd_a, twist, fwd_b, inv_b, inv_a


def split(value):
    high = value.astype(BF16)
    low = (value - high.astype(F32)).astype(BF16)
    return high, low


def mul(left, right):
    return jnp.dot(left, right, preferred_element_type=F32)


def to_spectra(cols, fwd_a, twist, fwd_b):
    blocks, width = cols[0].shape
    data = jnp.concatenate(cols, 1)
    part = mul(fwd_a, jnp.concatenate([data, data], 0))
    t_re, t_im = twist[:, :width], twist[:, width:]
    rows = []
    for s in range(len(cols)):
        a_re = part[:blocks, s * width : (s + 1) * width]
        a_im = part[blocks:, s * width : (s + 1) * width]
        rows.append(jnp.concatenate([a_re * t_re - a_im * t_im, a_re * t_im + a_im * t_re], 1))
    high, low = split(jnp.concatenate(rows, 0))
    return mul(jnp.concatenate([high, low, high], 1), fwd_b)


def from_spectra(spec, twist, inv_b, inv_a, scale):
    blocks = twist.shape[0]
    width = twist.shape[1] // 2
    count = spec.shape[0] // blocks
    high, low = split(spec)
    part = mul(jnp.concatenate([high, low, high], 1), inv_b)
    t_re, t_im = twist[:, :width], twist[:, width:]
    cols = []
    for s in range(count):
        d_re = part[s * blocks : (s + 1) * blocks, :width]
        d_im = part[s * blocks : (s + 1) * blocks, width:]
        cols.append(jnp.concatenate([d_re * t_re + d_im * t_im, d_im * t_re - d_re * t_im], 0))
    high, low = split(jnp.concatenate(cols, 1))
    return mul(inv_a, jnp.concatenate([high, low, high], 0)) * scale


def gate_kernel(repeat, blocks, query, key_in, value, cotangent, taps, out_ref, *scratch):
    hold, sems = scratch[-2], scratch[-1]
    width = taps.shape[0]
    fils = width // blocks
    per = (2 * repeat + 1) * fils
    copies = []
    for i, source in enumerate((key_in, value, taps, cotangent, query)):
        copies.append(pltpu.make_async_copy(source, scratch[i], sems.at[i]))
        copies[-1].start()
    k_in, v_in, t_in, g_in, q_in = scratch[:5]

    def put(first, part):
        flipped = part.T
        for f in range(fils):
            hold[pl.ds(first + f, blocks, stride=per), :] = flipped[f * blocks : (f + 1) * blocks]

    def put_product(first, left, right):
        for c in range(repeat):
            at = slice(c * width, (c + 1) * width)
            prod = left[:, at].astype(F32) * right[:, at].astype(F32)
            put(first + c * fils, prod.astype(BF16).astype(F32))

    copies[0].wait()
    copies[1].wait()
    put_product(0, k_in, v_in)
    copies[2].wait()
    put(2 * repeat * fils, t_in[...].astype(F32))
    copies[3].wait()
    copies[4].wait()
    put_product(repeat * fils, g_in, q_in)
    out_ref[...] = hold[...].astype(BF16)


def take_columns(ref, hold, per, blocks):
    hold[...] = ref[...].astype(F32)
    return [hold[pl.ds(s, blocks, stride=per), :].astype(BF16) for s in range(per)]


def times(a, b):
    w = a.shape[1] // 2
    a_re, a_im, b_re, b_im = a[:, :w], a[:, w:], b[:, :w], b[:, w:]
    return jnp.concatenate([a_re * b_re - a_im * b_im, a_re * b_im + a_im * b_re], 1)


def times_conj(a, b):
    w = a.shape[1] // 2
    a_re, a_im, b_re, b_im = a[:, :w], a[:, w:], b[:, :w], b[:, w:]
    return jnp.concatenate([a_re * b_re + a_im * b_im, a_im * b_re - a_re * b_im], 1)


def core_kernel(repeat, scale, x_ref, fa, tw, fb, ib, ia, out_ref, hold):
    blocks = tw.shape[0]
    width = tw.shape[1] // 2
    per = x_ref.shape[0] // blocks
    fils = per // (2 * repeat + 1)
    step = fils * blocks
    spec = to_spectra(take_columns(x_ref, hold, per, blocks), fa[...], tw[...], fb[...])
    parts = [spec[s * step : (s + 1) * step] for s in range(2 * repeat + 1)]
    mixed, gated, taps = parts[:repeat], parts[repeat : 2 * repeat], parts[-1]
    cross = times_conj(gated[0], mixed[0])
    for s in range(1, repeat):
        cross = cross + times_conj(gated[s], mixed[s])
    prods = [times(m, taps) for m in mixed] + [times_conj(g, taps) for g in gated] + [cross]
    result = from_spectra(jnp.concatenate(prods, 0), tw[...], ib[...], ia[...], scale)
    for s in range(per):
        hold[pl.ds(s, blocks, stride=per), :] = result[:, s * width : (s + 1) * width]
    out_ref[...] = hold[...].astype(BF16)


def back_rows(rows, first, blocks, width):
    per = rows.shape[0] // blocks
    parts = [rows[pl.ds(first + f, blocks, stride=per), :] for f in range(width // blocks)]
    return jnp.concatenate(parts, 0).T


def taps_kernel(repeat, blocks, rows_ref, taps_ref, hold):
    width = taps_ref.shape[0]
    hold[...] = rows_ref[...].astype(F32)
    taps_ref[...] = back_rows(hold, 2 * repeat * (width // blocks), blocks, width).astype(BF16)


def grads_kernel(repeat, blocks, rows_ref, cot, value, key_in, grad_query, grad_key, grad_value, hold):
    width = cot.shape[0]
    fils = width // blocks
    hold[...] = rows_ref[...].astype(F32)
    for c in range(repeat):
        at = slice(c * width, (c + 1) * width)
        conv = back_rows(hold, c * fils, blocks, width)
        grad_query[:, at] = (cot[:, at].astype(F32) * conv).astype(BF16)
        back = back_rows(hold, (repeat + c) * fils, blocks, width)
        grad_key[:, at] = (back * value[:, at].astype(F32)).astype(BF16)
        grad_value[:, at] = (back * key_in[:, at].astype(F32)).astype(BF16)


def sum_kernel(part_ref, out_ref):
    rows = out_ref.shape[0]
    total = part_ref[:rows].astype(F32)
    for c in range(1, part_ref.shape[0] // rows):
        total = total + part_ref[c * rows : (c + 1) * rows].astype(F32)
    out_ref[...] = total


def local(query, key_in, value, cotangent, filter_raw):
    width, channels = query.shape
    blocks = lax.axis_size("seq")
    groups = lax.axis_size("chan")
    length = blocks * width
    filters = filter_raw.shape[1]
    repeat = channels // filters
    fils = filters // blocks
    per = (2 * repeat + 1) * fils
    scale = 1.0 / (length * math.sqrt(length))
    tables = [jnp.asarray(t) for t in make_tables(blocks, width)]
    params = pltpu.CompilerParams(vmem_limit_bytes=VMEM_LIMIT)
    packed = jax.ShapeDtypeStruct((blocks * per, width), BF16)
    hold = pltpu.VMEM((blocks * per, width), F32)

    def swap(array):
        shape = (blocks, per // fils, fils, width)
        moved = lax.all_to_all(array.reshape(shape), "seq", split_axis=0, concat_axis=0, tiled=True)
        return moved.reshape(array.shape)

    wide = pltpu.VMEM((width, channels), BF16)
    rows = pl.pallas_call(
        functools.partial(gate_kernel, repeat, blocks),
        out_shape=packed,
        in_specs=[pl.BlockSpec(memory_space=pl.ANY)] * 5,
        scratch_shapes=[wide, wide, pltpu.VMEM((width, filters), BF16), wide, wide, hold, pltpu.SemaphoreType.DMA((5,))],
        compiler_params=params,
        name="gate",
    )(query, key_in, value, cotangent, filter_raw)
    rows = pl.pallas_call(
        functools.partial(core_kernel, repeat, scale),
        out_shape=packed,
        scratch_shapes=[hold],
        compiler_params=params,
        name="core",
    )(swap(rows), *tables)
    rows = swap(rows)
    taps = pl.pallas_call(
        functools.partial(taps_kernel, repeat, blocks),
        out_shape=jax.ShapeDtypeStruct((width, filters), BF16),
        scratch_shapes=[hold],
        compiler_params=params,
        name="taps",
    )(rows)
    taps = lax.all_to_all(taps, "chan", split_axis=0, concat_axis=0, tiled=True)
    like = jax.ShapeDtypeStruct((width, channels), BF16)
    grads = pl.pallas_call(
        functools.partial(grads_kernel, repeat, blocks),
        out_shape=(like, like, like),
        scratch_shapes=[hold],
        compiler_params=params,
        name="grads",
    )(rows, cotangent, value, key_in)
    grad_filter = pl.pallas_call(
        sum_kernel,
        out_shape=jax.ShapeDtypeStruct((width // groups, filters), F32),
        compiler_params=params,
        name="grad_filter",
    )(taps)
    return (*grads, grad_filter)


def solution(mesh):
    placed = (
        P("seq", "chan"),
        P("seq", "chan"),
        P("seq", "chan"),
        P("seq", "chan"),
        P("seq", None),
    )
    return jax.shard_map(
        local,
        mesh=mesh,
        in_specs=placed,
        out_specs=(P("seq", "chan"), P("seq", "chan"), P("seq", "chan"), P(("seq", "chan"), None)),
        check_vma=False,
    )
```

time: 119 us -> 86.6 us (0.73)
  waiting for transfers between devices: 52.4 us -> 4.84 us
  blocking collectives: 20.8 us -> 62.9 us
  starting transfers between devices: 33.8 us -> 7.11 us
  Pallas kernels: 6.98 us -> 5.16 us
  local copies, waits for them, and re-layouts: 2.57 us -> 4.36 us
    all_to_all x4 -> x1, waiting for transfers between devices: 52.4 us -> 4.84 us  [local(): taps = lax.all_to_all(taps, 'chan', split_axis=0, concat_axis=0, tiled=True)]
    all_to_all x1 -> x2, blocking collectives: 20.8 us -> 62.9 us  [swap(): lax.all_to_all(array.reshape(shape), 'seq', split_axis=0, concat_axis=0,...]
    all_to_all x4 -> x1, starting transfers between devices: 33.8 us -> 7.11 us  [local(): taps = lax.all_to_all(taps, 'chan', split_axis=0, concat_axis=0, tiled=True)]
    pallas_call x6 -> x4, Pallas kernels: 6.37 us -> 4.55 us  [the longest x1 2.04 us: local(): pl.pallas_call(functools.partial(core_kernel, repeat, scale), out_shape=p...]
    unnamed x24 -> x26, local copies, waits for them, and re-layouts: 2.57 us -> 4.36 us
  transfers between devices with their start and end apart: 4 -> 1, of which waited for: 4 -> 1; matrix products, arithmetic and copies ran while one was open for 0% -> 0% of each run, Pallas kernels for 4% -> 1%
where the time goes in v2:
time: 86.6 us; the launch traced here: 85.1 us
  blocking collectives  62.9 us (73%)
  starting transfers between devices  7.11 us (8%)
  Pallas kernels  5.16 us (6%)
  waiting for transfers between devices  4.84 us (6%)
  local copies, waits for them, and re-layouts  4.36 us (5%)
    all_to_all x2, blocking collectives, swap(): lax.all_to_all(array.reshape(shape), 'seq', split_axis=0, concat_axis=0,...  62.9 us
    all_to_all x1, starting transfers between devices, local(): taps = lax.all_to_all(taps, 'chan', split_axis=0, concat_axis=0, tiled=True)  7.11 us
    all_to_all x1, waiting for transfers between devices, local(): taps = lax.all_to_all(taps, 'chan', split_axis=0, concat_axis=0, tiled=True)  4.84 us
    unnamed x26, local copies, waits for them, and re-layouts  4.36 us
    pallas_call x1, Pallas kernels, local(): pl.pallas_call(functools.partial(core_kernel, repeat, scale), out_shape=p...  2.04 us
  transfers between devices with their start and end apart: 1, of which 1 were waited for; matrix products, arithmetic and copies ran while one was open for 0% of the time, Pallas kernels for 1%

profile of v2, /device:TPU:6, one launch (start us, length us, event | category | flops | bytes accessed | tf_op | source)
XLA Modules:
  0.0 85.1 jit_solution(16590187066687047548)
XLA Ops:
  0.6 0.0 copy-start
  0.6 0.9 %copy-done = bf16[128,384]{1,0:T(8,128)(2,1)S(1)} copy-done((bf16[128,384]{1,0:T(8,128)(2,1)S(1)}, bf16[128,384]{1,0:T(8,128)(2,1)}, u32[]{:S(2)}) %copy-start) | copy-done | bytes 98328
  1.5 0.0 copy-start.2
  1.5 0.9 %copy-done.2 = bf16[128,384]{1,0:T(8,128)(2,1)S(1)} copy-done((bf16[128,384]{1,0:T(8,128)(2,1)S(1)}, bf16[128,384]{1,0:T(8,128)(2,1)}, u32[]{:S(2)}) %copy-start.2) | copy-done | bytes 98328
  2.4 0.0 copy-start.4
  2.4 0.9 %copy-done.4 = bf16[128,384]{1,0:T(8,128)(2,1)S(1)} copy-done((bf16[128,384]{1,0:T(8,128)(2,1)S(1)}, bf16[128,384]{1,0:T(8,128)(2,1)}, u32[]{:S(2)}) %copy-start.4) | copy-done | bytes 98328
  3.3 0.0 copy-start.8
  3.3 0.9 %copy-done.8 = bf16[128,384]{1,0:T(8,128)(2,1)S(1)} copy-done((bf16[128,384]{1,0:T(8,128)(2,1)S(1)}, bf16[128,384]{1,0:T(8,128)(2,1)}, u32[]{:S(2)}) %copy-start.8) | copy-done | bytes 98328
  4.2 0.0 copy-start.11
  4.2 0.8 copy-done.11
  5.0 0.0 copy-start.7
  5.0 0.0 copy-start.10
  5.0 0.0 copy-start.12
  5.0 0.9 %gate.1 = bf16[896,128]{1,0:T(8,128)(2,1)S(1)} custom-call(bf16[128,384]{1,0:T(8,128)(2,1)S(1)} %copy-done.8, bf16[128,384]{1,0:T(8,128)(2,1)S(1)} %copy-done, bf16[128,384]{1,0:T(8,128)(2,1)S(1)} %copy-done.2, bf16[128,384]{1,0:T(8,128)(2,1)S(1)} %copy-done.4, bf16[128,128]{1,0:T(8,128)(2,1)S(1)} %copy-done.11), custom_call_target="tpu_custom_call" | custom-call | tf_op jit(solution)/shard_map/gate/pallas_call | solution.py:208
  5.9 0.0 copy-start.6
  5.9 0.0 copy-start.9
  5.9 38.1 %all_to_all.21 = bf16[64,7,2,128]{3,2,1,0:T(2,128)(2,1)S(1)} all-to-all(bf16[64,7,2,128]{3,2,1,0:T(2,128)(2,1)S(1)} %bitcast.8), channel_id=1, replica_groups=mesh['seq'=64,'chan'=8] {'seq'}, dimensions={0} | all-to-all | bytes 458752 | tf_op jit(solution)/shard_map/all_to_all | solution.py:204
  44.0 0.0 copy-done.7
  44.0 0.0 copy-done.10
  44.0 0.0 copy-done.12
  44.0 0.0 copy-done.6
  44.0 0.0 copy-done.9
  44.0 2.0 %core.1 = bf16[896,128]{1,0:T(8,128)(2,1)S(1)} custom-call(bf16[896,128]{1,0:T(8,128)(2,1)S(1)} %bitcast.9, bf16[128,128]{1,0:T(8,128)(2,1)S(1)} %copy-done.12, f32[64,256]{1,0:T(8,128)S(1)} %copy-done.9, bf16[768,256]{1,0:T(8,128)(2,1)S(1)} %copy-done.7, bf16[768,256]{1,0:T(8,128)(2,1)S(1)} %copy-done.6, bf16[64,384]{1,0:T(8,128)(2,1)S(1)} %copy-done.10), custom_call_target="tpu_custom_call" | custom-call | tf_op jit(solution)/shard_map/core/pallas_call | solution.py:216
  46.1 24.8 %all_to_all.22 = bf16[64,7,2,128]{3,2,1,0:T(2,128)(2,1)S(1)} all-to-all(bf16[64,7,2,128]{3,2,1,0:T(2,128)(2,1)S(1)} %bitcast.10), channel_id=1, replica_groups=mesh['seq'=64,'chan'=8] {'seq'}, dimensions={0} | all-to-all | bytes 458752 | tf_op jit(solution)/shard_map/all_to_all | solution.py:204
  70.9 0.0 copy-start.1
  70.9 0.0 copy-start.3
  70.9 0.0 copy-start.5
  70.9 0.7 taps.3
  71.6 7.1 %all-to-all-start.2 = ((bf16[8,16,128]{2,1,0:T(8,128)(2,1)}), bf16[8,16,128]{2,1,0:T(8,128)(2,1)S(1)}, u32[]{:S(2)}, u32[]{:S(2)}) async-start(bf16[8,16,128]{2,1,0:T(8,128)(2,1)} %bitcast.4), calls=%async_computation.2 | async-start | bytes 65536 | tf_op jit(solution)/shard_map/all_to_all | solution.py:231
  78.7 0.0 copy-done.1
  78.7 0.0 copy-done.3
  78.7 0.0 copy-done.5
  78.7 0.9 %grads.1 = (bf16[128,384]{1,0:T(8,128)(2,1)}, bf16[128,384]{1,0:T(8,128)(2,1)}, bf16[128,384]{1,0:T(8,128)(2,1)}) custom-call(bf16[896,128]{1,0:T(8,128)(2,1)S(1)} %bitcast.7, bf16[128,384]{1,0:T(8,128)(2,1)S(1)} %copy-done.5, bf16[128,384]{1,0:T(8,128)(2,1)S(1)} %copy-done.3, bf16[128,384]{1,0:T(8,128)(2,1)S(1)} %copy-done.1), custom_call_target="tpu_custom_call" | custom-call | tf_op jit(solution)/shard_map/grads/pallas_call | solution.py:233
  79.6 4.8 %all-to-all-done.2 = bf16[8,16,128]{2,1,0:T(8,128)(2,1)S(1)} async-done(((bf16[8,16,128]{2,1,0:T(8,128)(2,1)}), bf16[8,16,128]{2,1,0:T(8,128)(2,1)S(1)}, u32[]{:S(2)}, u32[]{:S(2)}) %all-to-all-start.2) | async-done | bytes 32800 | tf_op jit(solution)/shard_map/all_to_all | solution.py:231
  84.5 0.6 grad_filter.1
Async XLA Ops:
  0.6 0.9 %copy-start = (bf16[128,384]{1,0:T(8,128)(2,1)S(1)}, bf16[128,384]{1,0:T(8,128)(2,1)}, u32[]{:S(2)}) copy-start(bf16[128,384]{1,0:T(8,128)(2,1)} %key_in.3) | copy-start | bytes 294916
  1.5 0.9 %copy-start.2 = (bf16[128,384]{1,0:T(8,128)(2,1)S(1)}, bf16[128,384]{1,0:T(8,128)(2,1)}, u32[]{:S(2)}) copy-start(bf16[128,384]{1,0:T(8,128)(2,1)} %value.3) | copy-start | bytes 294916
  2.4 0.9 %copy-start.4 = (bf16[128,384]{1,0:T(8,128)(2,1)S(1)}, bf16[128,384]{1,0:T(8,128)(2,1)}, u32[]{:S(2)}) copy-start(bf16[128,384]{1,0:T(8,128)(2,1)} %cot.1) | copy-start | bytes 294916
  3.3 0.9 %copy-start.8 = (bf16[128,384]{1,0:T(8,128)(2,1)S(1)}, bf16[128,384]{1,0:T(8,128)(2,1)}, u32[]{:S(2)}) copy-start(bf16[128,384]{1,0:T(8,128)(2,1)} %query.1) | copy-start | bytes 294916
  4.2 0.8 copy-start.11
  5.0 39.0 %copy-start.7 = (bf16[768,256]{1,0:T(8,128)(2,1)S(1)}, bf16[768,256]{1,0:T(8,128)(2,1)}, u32[]{:S(2)}) copy-start(bf16[768,256]{1,0:T(8,128)(2,1)} %constant.12.clone.fb) | copy-start | bytes 1179652
  5.0 39.0 %copy-start.10 = (bf16[64,384]{1,0:T(8,128)(2,1)S(1)}, bf16[64,384]{1,0:T(8,128)(2,1)}, u32[]{:S(2)}) copy-start(bf16[64,384]{1,0:T(8,128)(2,1)} %constant.14.clone.ia) | copy-start | bytes 147460
  5.0 39.0 %copy-start.12 = (bf16[128,128]{1,0:T(8,128)(2,1)S(1)}, bf16[128,128]{1,0:T(8,128)(2,1)}, u32[]{:S(2)}) copy-start(bf16[128,128]{1,0:T(8,128)(2,1)} %constant.10.clone.fa) | copy-start | bytes 98308
  5.9 38.1 %copy-start.6 = (bf16[768,256]{1,0:T(8,128)(2,1)S(1)}, bf16[768,256]{1,0:T(8,128)(2,1)}, u32[]{:S(2)}) copy-start(bf16[768,256]{1,0:T(8,128)(2,1)} %constant.13.clone.ib) | copy-start | bytes 1179652
  5.9 38.1 %copy-start.9 = (f32[64,256]{1,0:T(8,128)S(1)}, f32[64,256]{1,0:T(8,128)}, u32[]{:S(2)}) copy-start(f32[64,256]{1,0:T(8,128)} %constant.11.clone.tw) | copy-start | bytes 196612
  70.9 7.8 %copy-start.1 = (bf16[128,384]{1,0:T(8,128)(2,1)S(1)}, bf16[128,384]{1,0:T(8,128)(2,1)}, u32[]{:S(2)}) copy-start(bf16[128,384]{1,0:T(8,128)(2,1)} %key_in.3) | copy-start | bytes 294916
  70.9 7.8 %copy-start.3 = (bf16[128,384]{1,0:T(8,128)(2,1)S(1)}, bf16[128,384]{1,0:T(8,128)(2,1)}, u32[]{:S(2)}) copy-start(bf16[128,384]{1,0:T(8,128)(2,1)} %value.3) | copy-start | bytes 294916
  70.9 7.8 %copy-start.5 = (bf16[128,384]{1,0:T(8,128)(2,1)S(1)}, bf16[128,384]{1,0:T(8,128)(2,1)}, u32[]{:S(2)}) copy-start(bf16[128,384]{1,0:T(8,128)(2,1)} %cot.1) | copy-start | bytes 294916
  71.6 12.9 %all-to-all-start.2 = ((bf16[8,16,128]{2,1,0:T(8,128)(2,1)}), bf16[8,16,128]{2,1,0:T(8,128)(2,1)S(1)}, u32[]{:S(2)}, u32[]{:S(2)}) async-start(bf16[8,16,128]{2,1,0:T(8,128)(2,1)} %bitcast.4), calls=%async_computation.2 | async-start | bytes 65536 | tf_op jit(solution)/shard_map/all_to_all | solution.py:231

commit v3 on v2

--- a/solution.py
+++ b/solution.py
@@ -20,9 +20,9 @@
     return high, low
 
 
-def make_tables(blocks, width):
+def make_tables(blocks, width, order):
     length = blocks * width
-    j = np.arange(blocks)
+    j = np.array(order)
     k1 = np.arange(blocks) + 0.25
     r = np.arange(width)
     k2 = np.arange(width)
@@ -157,16 +157,14 @@
     return jnp.concatenate(parts, 0).T
 
 
-def taps_kernel(repeat, blocks, rows_ref, taps_ref, hold):
-    width = taps_ref.shape[0]
-    hold[...] = rows_ref[...].astype(F32)
-    taps_ref[...] = back_rows(hold, 2 * repeat * (width // blocks), blocks, width).astype(BF16)
-
-
-def grads_kernel(repeat, blocks, rows_ref, cot, value, key_in, grad_query, grad_key, grad_value, hold):
+def grads_kernel(repeat, blocks, group, rows_ref, cot, value, key_in, grad_query, grad_key, grad_value, taps, hold):
     width = cot.shape[0]
     fils = width // blocks
     hold[...] = rows_ref[...].astype(F32)
+    flipped = back_rows(hold, 2 * repeat * fils, blocks, width).astype(BF16)
+    lags = width // len(group)
+    for c, owner in enumerate(group):
+        taps[c * lags : (c + 1) * lags] = flipped[owner * lags : (owner + 1) * lags]
     for c in range(repeat):
         at = slice(c * width, (c + 1) * width)
         conv = back_rows(hold, c * fils, blocks, width)
@@ -194,14 +192,17 @@
     fils = filters // blocks
     per = (2 * repeat + 1) * fils
     scale = 1.0 / (length * math.sqrt(length))
-    tables = [jnp.asarray(t) for t in make_tables(blocks, width)]
+    first = blocks // 2 + 2
+    group = [(3 * groups // 4 + c) % groups for c in range(groups)]
+    order = [(first + i) % blocks for i in range(blocks)]
+    tables = [jnp.asarray(t) for t in make_tables(blocks, width, order)]
     params = pltpu.CompilerParams(vmem_limit_bytes=VMEM_LIMIT)
     packed = jax.ShapeDtypeStruct((blocks * per, width), BF16)
     hold = pltpu.VMEM((blocks * per, width), F32)
 
     def swap(array):
         shape = (blocks, per // fils, fils, width)
-        moved = lax.all_to_all(array.reshape(shape), "seq", split_axis=0, concat_axis=0, tiled=True)
+        moved = lax.all_to_all(array.reshape(shape), "seq", split_axis=0, concat_axis=0, tiled=True, axis_index_groups=[order])
         return moved.reshape(array.shape)
 
     wide = pltpu.VMEM((width, channels), BF16)
@@ -210,7 +211,6 @@
         out_shape=packed,
         in_specs=[pl.BlockSpec(memory_space=pl.ANY)] * 5,
         scratch_shapes=[wide, wide, pltpu.VMEM((width, filters), BF16), wide, wide, hold, pltpu.SemaphoreType.DMA((5,))],
-        compiler_params=params,
         name="gate",
     )(query, key_in, value, cotangent, filter_raw)
     rows = pl.pallas_call(
@@ -221,22 +221,15 @@
         name="core",
     )(swap(rows), *tables)
     rows = swap(rows)
-    taps = pl.pallas_call(
-        functools.partial(taps_kernel, repeat, blocks),
-        out_shape=jax.ShapeDtypeStruct((width, filters), BF16),
-        scratch_shapes=[hold],
-        compiler_params=params,
-        name="taps",
-    )(rows)
-    taps = lax.all_to_all(taps, "chan", split_axis=0, concat_axis=0, tiled=True)
     like = jax.ShapeDtypeStruct((width, channels), BF16)
-    grads = pl.pallas_call(
-        functools.partial(grads_kernel, repeat, blocks),
-        out_shape=(like, like, like),
+    *grads, taps = pl.pallas_call(
+        functools.partial(grads_kernel, repeat, blocks, group),
+        out_shape=(like, like, like, jax.ShapeDtypeStruct((width, filters), BF16)),
         scratch_shapes=[hold],
         compiler_params=params,
         name="grads",
     )(rows, cotangent, value, key_in)
+    taps = lax.all_to_all(taps, "chan", split_axis=0, concat_axis=0, tiled=True, axis_index_groups=[group])
     grad_filter = pl.pallas_call(
         sum_kernel,
         out_shape=jax.ShapeDtypeStruct((width // groups, filters), F32),

time: 86.6 us -> 73.9 us (0.85); the launches traced: 85.1 us -> 73.5 us
  starting transfers between devices: 7.11 us -> 0 us
  waiting for transfers between devices: 4.84 us -> 0 us
  local copies, waits for them, and re-layouts: 4.36 us -> 0.05 us
  blocking collectives: 62.9 us -> 67.1 us
    all_to_all x0 -> x1, blocking collectives: none -> 10.2 us  [local(): lax.all_to_all(taps, 'chan', split_axis=0, concat_axis=0, tiled=True, axi...]
    all_to_all x1 -> x0, starting transfers between devices: 7.11 us -> none  [local(): taps = lax.all_to_all(taps, 'chan', split_axis=0, concat_axis=0, tiled=True)]
    all_to_all x2, blocking collectives: 62.9 us -> 56.9 us  [swap(): lax.all_to_all(array.reshape(shape), 'seq', split_axis=0, concat_axis=0,...]
    all_to_all x1 -> x0, waiting for transfers between devices: 4.84 us -> none  [local(): taps = lax.all_to_all(taps, 'chan', split_axis=0, concat_axis=0, tiled=True)]
    unnamed x26 -> x16, local copies, waits for them, and re-layouts: 4.36 us -> 0.05 us
    pallas_call x1, Pallas kernels: 0.92 us -> 2.05 us  [local(): pl.pallas_call(functools.partial(gate_kernel, repeat, blocks), out_shape=...]
  transfers between devices with their start and end apart: 1 -> 0, of which waited for: 1 -> 0; matrix products, arithmetic and copies ran while one was open for 0% -> 0% of each run, Pallas kernels for 1% -> 0%
where the time goes in v3:
time: 73.9 us; the launch traced here: 73.5 us
  blocking collectives  67.1 us (91%)
  Pallas kernels  5.58 us (8%)
  between operations  0.74 us (1%)
    all_to_all x2, blocking collectives, swap(): lax.all_to_all(array.reshape(shape), 'seq', split_axis=0, concat_axis=0,...  56.9 us
    all_to_all x1, blocking collectives, local(): lax.all_to_all(taps, 'chan', split_axis=0, concat_axis=0, tiled=True, axi...  10.2 us
    pallas_call x1, Pallas kernels, local(): pl.pallas_call(functools.partial(gate_kernel, repeat, blocks), out_shape=...  2.05 us
    pallas_call x1, Pallas kernels, local(): pl.pallas_call(functools.partial(core_kernel, repeat, scale), out_shape=p...  2.03 us

profile of v3, /device:TPU:6, one launch (start us, length us, event | category | flops | bytes accessed | tf_op | source)
XLA Modules:
  0.0 73.5 jit_solution(16434498157161200565)
XLA Ops:
  0.6 0.0 copy-start.4
  0.6 0.0 copy-start.6
  0.7 0.0 copy-start.7
  0.7 2.1 %gate.1 = bf16[896,128]{1,0:T(8,128)(2,1)} custom-call(bf16[128,384]{1,0:T(8,128)(2,1)} %query.1, bf16[128,384]{1,0:T(8,128)(2,1)} %key_in.3, bf16[128,384]{1,0:T(8,128)(2,1)} %value.3, bf16[128,384]{1,0:T(8,128)(2,1)} %cot.1, bf16[128,128]{1,0:T(8,128)(2,1)} %taps.1), custom_call_target="tpu_custom_call" | custom-call | tf_op jit(solution)/shard_map/gate/pallas_call | solution.py:209
  2.7 0.0 copy-start.3
  2.7 0.0 copy-start.5
  2.8 31.9 %all_to_all.21 = bf16[64,7,2,128]{3,2,1,0:T(2,128)(2,1)S(1)} all-to-all(bf16[64,7,2,128]{3,2,1,0:T(2,128)(2,1)} %bitcast.11), channel_id=1, replica_groups={{272,280,288,296,304,312,320,328,336,344,352,360,368,376,384,392,400,40..., dimensions={0} | all-to-all | bytes 458752 | tf_op jit(solution)/shard_map/all_to_all | solution.py:205
  34.7 0.0 copy-done.4
  34.7 0.0 copy-done.6
  34.7 0.0 copy-done.7
  34.7 0.0 copy-done.3
  34.7 0.0 copy-done.5
  34.7 2.0 %core.1 = bf16[896,128]{1,0:T(8,128)(2,1)S(1)} custom-call(bf16[896,128]{1,0:T(8,128)(2,1)S(1)} %bitcast.7, bf16[128,128]{1,0:T(8,128)(2,1)S(1)} %copy-done.7, f32[64,256]{1,0:T(8,128)S(1)} %copy-done.5, bf16[768,256]{1,0:T(8,128)(2,1)S(1)} %copy-done.4, bf16[768,256]{1,0:T(8,128)(2,1)S(1)} %copy-done.3, bf16[64,384]{1,0:T(8,128)(2,1)S(1)} %copy-done.6), custom_call_target="tpu_custom_call" | custom-call | tf_op jit(solution)/shard_map/core/pallas_call | solution.py:216
  36.8 0.0 copy-start
  36.8 0.0 copy-start.1
  36.8 0.0 copy-start.2
  36.8 25.0 %all_to_all.22 = bf16[64,7,2,128]{3,2,1,0:T(2,128)(2,1)S(1)} all-to-all(bf16[64,7,2,128]{3,2,1,0:T(2,128)(2,1)S(1)} %bitcast.8), channel_id=1, replica_groups={{272,280,288,296,304,312,320,328,336,344,352,360,368,376,384,392,400,40..., dimensions={0} | all-to-all | bytes 458752 | tf_op jit(solution)/shard_map/all_to_all | solution.py:205
  61.8 0.0 copy-done
  61.8 0.0 copy-done.1
  61.8 0.0 copy-done.2
  61.8 0.9 %grads.1 = (bf16[128,384]{1,0:T(8,128)(2,1)}, bf16[128,384]{1,0:T(8,128)(2,1)}, bf16[128,384]{1,0:T(8,128)(2,1)}, bf16[128,128]{1,0:T(8,128)(2,1)S(1)}) custom-call(bf16[896,128]{1,0:T(8,128)(2,1)S(1)} %bitcast.6, bf16[128,384]{1,0:T(8,128)(2,1)S(1)} %copy-done.2, bf16[128,384]{1,0:T(8,128)(2,1)S(1)} %copy-done.1, bf16[128,384]{1,0:T(8,128)(2,1)S(1)} %copy-done), custom_call_target="tpu_custom_call" | custom-call | tf_op jit(solution)/shard_map/grads/pallas_call | solution.py:225
  62.7 10.2 %all_to_all.23 = bf16[8,16,128]{2,1,0:T(8,128)(2,1)S(1)} all-to-all(bf16[8,16,128]{2,1,0:T(8,128)(2,1)S(1)} %bitcast.10), channel_id=1, replica_groups={{6,7,0,1,2,3,4,5},{14,15,8,9,10,11,12,13},{22,23,16,17,18,19,20,21},{30..., dimensions={0} | all-to-all | bytes 65536 | tf_op jit(solution)/shard_map/all_to_all | solution.py:232
  72.9 0.6 grad_filter.1
Async XLA Ops:
  0.6 34.1 %copy-start.4 = (bf16[768,256]{1,0:T(8,128)(2,1)S(1)}, bf16[768,256]{1,0:T(8,128)(2,1)}, u32[]{:S(2)}) copy-start(bf16[768,256]{1,0:T(8,128)(2,1)} %constant.12.clone.fb) | copy-start | bytes 1179652
  0.6 34.0 %copy-start.6 = (bf16[64,384]{1,0:T(8,128)(2,1)S(1)}, bf16[64,384]{1,0:T(8,128)(2,1)}, u32[]{:S(2)}) copy-start(bf16[64,384]{1,0:T(8,128)(2,1)} %constant.14.clone.ia) | copy-start | bytes 147460
  0.7 34.0 %copy-start.7 = (bf16[128,128]{1,0:T(8,128)(2,1)S(1)}, bf16[128,128]{1,0:T(8,128)(2,1)}, u32[]{:S(2)}) copy-start(bf16[128,128]{1,0:T(8,128)(2,1)} %constant.10.clone.fa) | copy-start | bytes 98308
  2.7 32.0 %copy-start.3 = (bf16[768,256]{1,0:T(8,128)(2,1)S(1)}, bf16[768,256]{1,0:T(8,128)(2,1)}, u32[]{:S(2)}) copy-start(bf16[768,256]{1,0:T(8,128)(2,1)} %constant.13.clone.ib) | copy-start | bytes 1179652
  2.7 32.0 %copy-start.5 = (f32[64,256]{1,0:T(8,128)S(1)}, f32[64,256]{1,0:T(8,128)}, u32[]{:S(2)}) copy-start(f32[64,256]{1,0:T(8,128)} %constant.11.clone.tw) | copy-start | bytes 196612
  36.8 25.0 %copy-start = (bf16[128,384]{1,0:T(8,128)(2,1)S(1)}, bf16[128,384]{1,0:T(8,128)(2,1)}, u32[]{:S(2)}) copy-start(bf16[128,384]{1,0:T(8,128)(2,1)} %key_in.3) | copy-start | bytes 294916
  36.8 25.0 %copy-start.1 = (bf16[128,384]{1,0:T(8,128)(2,1)S(1)}, bf16[128,384]{1,0:T(8,128)(2,1)}, u32[]{:S(2)}) copy-start(bf16[128,384]{1,0:T(8,128)(2,1)} %value.3) | copy-start | bytes 294916
  36.8 25.0 %copy-start.2 = (bf16[128,384]{1,0:T(8,128)(2,1)S(1)}, bf16[128,384]{1,0:T(8,128)(2,1)}, u32[]{:S(2)}) copy-start(bf16[128,384]{1,0:T(8,128)(2,1)} %cot.1) | copy-start | bytes 294916

commit v4 on v3

--- a/solution.py
+++ b/solution.py
@@ -37,9 +37,7 @@
     b_hi, b_lo = split_table(inner_t)
     fwd_a = np.concatenate([a_hi, a_lo], 1)
     fwd_b = np.concatenate([b_hi, b_hi, b_lo], 0)
-    inv_b = np.concatenate([b_hi.T, b_hi.T, b_lo.T], 0)
-    inv_a = np.concatenate([a_hi.T, a_hi.T, a_lo.T], 1)
-    return fwd_a, twist, fwd_b, inv_b, inv_a
+    return fwd_a, twist, fwd_b, b_hi.T, a_hi.T
 
 
 def split(value):
@@ -70,16 +68,14 @@
     blocks = twist.shape[0]
     width = twist.shape[1] // 2
     count = spec.shape[0] // blocks
-    high, low = split(spec)
-    part = mul(jnp.concatenate([high, low, high], 1), inv_b)
+    part = mul(spec.astype(BF16), inv_b)
     t_re, t_im = twist[:, :width], twist[:, width:]
     cols = []
     for s in range(count):
         d_re = part[s * blocks : (s + 1) * blocks, :width]
         d_im = part[s * blocks : (s + 1) * blocks, width:]
         cols.append(jnp.concatenate([d_re * t_re + d_im * t_im, d_im * t_re - d_re * t_im], 0))
-    high, low = split(jnp.concatenate(cols, 1))
-    return mul(inv_a, jnp.concatenate([high, low, high], 0)) * scale
+    return mul(inv_a, jnp.concatenate(cols, 1).astype(BF16)) * scale
 
 
 def gate_kernel(repeat, blocks, query, key_in, value, cotangent, taps, out_ref, *scratch):
@@ -157,14 +153,26 @@
     return jnp.concatenate(parts, 0).T
 
 
-def grads_kernel(repeat, blocks, group, rows_ref, cot, value, key_in, grad_query, grad_key, grad_value, taps, hold):
+def taps_kernel(repeat, blocks, group, rows_ref, taps, hold):
+    width = taps.shape[1]
+    hold[...] = rows_ref[...].astype(F32)
+    flipped = back_rows(hold, 2 * repeat * (width // blocks), blocks, width).astype(BF16)
+    lags = width // len(group)
+    for c, owner in enumerate(group):
+        taps[c * lags : (c + 1) * lags] = flipped[owner * lags : (owner + 1) * lags]
+
+
+def grads_kernel(
+    repeat, blocks, rows_ref, part_ref, cot, value, key_in, grad_query, grad_key, grad_value, grad_filter, hold
+):
     width = cot.shape[0]
     fils = width // blocks
     hold[...] = rows_ref[...].astype(F32)
-    flipped = back_rows(hold, 2 * repeat * fils, blocks, width).astype(BF16)
-    lags = width // len(group)
-    for c, owner in enumerate(group):
-        taps[c * lags : (c + 1) * lags] = flipped[owner * lags : (owner + 1) * lags]
+    lags = grad_filter.shape[0]
+    total = part_ref[:lags].astype(F32)
+    for c in range(1, width // lags):
+        total = total + part_ref[c * lags : (c + 1) * lags].astype(F32)
+    grad_filter[...] = total
     for c in range(repeat):
         at = slice(c * width, (c + 1) * width)
         conv = back_rows(hold, c * fils, blocks, width)
@@ -172,14 +180,6 @@
         back = back_rows(hold, (repeat + c) * fils, blocks, width)
         grad_key[:, at] = (back * value[:, at].astype(F32)).astype(BF16)
         grad_value[:, at] = (back * key_in[:, at].astype(F32)).astype(BF16)
-
-
-def sum_kernel(part_ref, out_ref):
-    rows = out_ref.shape[0]
-    total = part_ref[:rows].astype(F32)
-    for c in range(1, part_ref.shape[0] // rows):
-        total = total + part_ref[c * rows : (c + 1) * rows].astype(F32)
-    out_ref[...] = total
 
 
 def local(query, key_in, value, cotangent, filter_raw):
@@ -211,8 +211,9 @@
         out_shape=packed,
         in_specs=[pl.BlockSpec(memory_space=pl.ANY)] * 5,
         scratch_shapes=[wide, wide, pltpu.VMEM((width, filters), BF16), wide, wide, hold, pltpu.SemaphoreType.DMA((5,))],
+        compiler_params=params,
         name="gate",
-    )(query, key_in, value, cotangent, filter_raw)
+    )(*(pltpu.with_memory_space_constraint(a, pltpu.HBM) for a in (query, key_in, value, cotangent, filter_raw)))
     rows = pl.pallas_call(
         functools.partial(core_kernel, repeat, scale),
         out_shape=packed,
@@ -222,21 +223,21 @@
     )(swap(rows), *tables)
     rows = swap(rows)
     like = jax.ShapeDtypeStruct((width, channels), BF16)
-    *grads, taps = pl.pallas_call(
-        functools.partial(grads_kernel, repeat, blocks, group),
-        out_shape=(like, like, like, jax.ShapeDtypeStruct((width, filters), BF16)),
+    taps = pl.pallas_call(
+        functools.partial(taps_kernel, repeat, blocks, group),
+        out_shape=jax.ShapeDtypeStruct((width, filters), BF16),
         scratch_shapes=[hold],
         compiler_params=params,
+        name="taps",
+    )(rows)
+    taps = lax.all_to_all(taps, "chan", split_axis=0, concat_axis=0, tiled=True, axis_index_groups=[group])
+    return pl.pallas_call(
+        functools.partial(grads_kernel, repeat, blocks),
+        out_shape=(like, like, like, jax.ShapeDtypeStruct((width // groups, filters), F32)),
+        scratch_shapes=[hold],
+        compiler_params=params,
         name="grads",
-    )(rows, cotangent, value, key_in)
-    taps = lax.all_to_all(taps, "chan", split_axis=0, concat_axis=0, tiled=True, axis_index_groups=[group])
-    grad_filter = pl.pallas_call(
-        sum_kernel,
-        out_shape=jax.ShapeDtypeStruct((width // groups, filters), F32),
-        compiler_params=params,
-        name="grad_filter",
-    )(taps)
-    return (*grads, grad_filter)
+    )(rows, taps, cotangent, value, key_in)
 
 
 def solution(mesh):

time: 73.9 us -> 72 us (0.974)
  Pallas kernels: 5.58 us -> 3.84 us
where the time goes in v4:
time: 72 us; the launch traced here: 71.5 us
  blocking collectives  66.9 us (93%)
  Pallas kernels  3.84 us (5%)
  between operations  0.72 us (1%)
    all_to_all x2, blocking collectives, swap(): lax.all_to_all(array.reshape(shape), 'seq', split_axis=0, concat_axis=0,...  56.6 us
    all_to_all x1, blocking collectives, local(): lax.all_to_all(taps, 'chan', split_axis=0, concat_axis=0, tiled=True, axi...  10.3 us
    pallas_call x1, Pallas kernels, local(): pl.pallas_call(functools.partial(core_kernel, repeat, scale), out_shape=p...  1.47 us

profile of v4, /device:TPU:6, one launch (start us, length us, event | category | flops | bytes accessed | tf_op | source)
XLA Modules:
  0.0 71.5 jit_solution(5162597073227490680)
XLA Ops:
  0.6 0.0 copy-start.4
  0.6 0.0 copy-start.6
  0.7 0.0 copy-start.7
  0.7 1.4 %gate.1 = bf16[896,128]{1,0:T(8,128)(2,1)S(1)} custom-call(bf16[128,384]{1,0:T(8,128)(2,1)} %query.1, bf16[128,384]{1,0:T(8,128)(2,1)} %key_in.3, bf16[128,384]{1,0:T(8,128)(2,1)} %value.3, bf16[128,384]{1,0:T(8,128)(2,1)} %cot.1, bf16[128,128]{1,0:T(8,128)(2,1)} %taps.2), custom_call_target="tpu_custom_call" | custom-call | tf_op jit(solution)/shard_map/gate/pallas_call | solution.py:209
  2.1 0.0 copy-start
  2.1 0.0 copy-start.5
  2.1 31.7 %all_to_all.21 = bf16[64,7,2,128]{3,2,1,0:T(2,128)(2,1)S(1)} all-to-all(bf16[64,7,2,128]{3,2,1,0:T(2,128)(2,1)S(1)} %bitcast.10), channel_id=1, replica_groups={{272,280,288,296,304,312,320,328,336,344,352,360,368,376,384,392,400,40..., dimensions={0} | all-to-all | bytes 458752 | tf_op jit(solution)/shard_map/all_to_all | solution.py:205
  33.8 0.0 copy-done.4
  33.8 0.0 copy-done.6
  33.8 0.0 copy-done.7
  33.8 0.0 copy-done
  33.8 0.0 copy-done.5
  33.8 1.5 %core.1 = bf16[896,128]{1,0:T(8,128)(2,1)S(1)} custom-call(bf16[896,128]{1,0:T(8,128)(2,1)S(1)} %bitcast.8, bf16[128,128]{1,0:T(8,128)(2,1)S(1)} %copy-done.6, f32[64,256]{1,0:T(8,128)S(1)} %copy-done.5, bf16[768,256]{1,0:T(8,128)(2,1)S(1)} %copy-done, bf16[256,256]{1,0:T(8,128)(2,1)S(1)} %copy-done.4, bf16[64,128]{1,0:T(8,128)(2,1)S(1)} %copy-done.7), custom_call_target="tpu_custom_call" | custom-call | tf_op jit(solution)/shard_map/core/pallas_call | solution.py:217
  35.3 24.8 %all_to_all.22 = bf16[64,7,2,128]{3,2,1,0:T(2,128)(2,1)S(1)} all-to-all(bf16[64,7,2,128]{3,2,1,0:T(2,128)(2,1)S(1)} %bitcast.9), channel_id=1, replica_groups={{272,280,288,296,304,312,320,328,336,344,352,360,368,376,384,392,400,40..., dimensions={0} | all-to-all | bytes 458752 | tf_op jit(solution)/shard_map/all_to_all | solution.py:205
  60.1 0.0 copy-start.1
  60.1 0.0 copy-start.2
  60.2 0.0 copy-start.3
  60.2 0.1 taps.3
  60.3 10.3 %all_to_all.23 = bf16[8,16,128]{2,1,0:T(8,128)(2,1)S(1)} all-to-all(bf16[8,16,128]{2,1,0:T(8,128)(2,1)S(1)} %bitcast.12), channel_id=1, replica_groups={{6,7,0,1,2,3,4,5},{14,15,8,9,10,11,12,13},{22,23,16,17,18,19,20,21},{30..., dimensions={0} | all-to-all | bytes 65536 | tf_op jit(solution)/shard_map/all_to_all | solution.py:233
  70.6 0.0 copy-done.1
  70.6 0.0 copy-done.2
  70.6 0.0 copy-done.3
  70.6 0.9 %grads.1 = (bf16[128,384]{1,0:T(8,128)(2,1)}, bf16[128,384]{1,0:T(8,128)(2,1)}, bf16[128,384]{1,0:T(8,128)(2,1)}, f32[16,128]{1,0:T(8,128)}) custom-call(bf16[896,128]{1,0:T(8,128)(2,1)S(1)} %bitcast.7, bf16[128,128]{1,0:T(8,128)(2,1)S(1)} %bitcast.11, bf16[128,384]{1,0:T(8,128)(2,1)S(1)} %copy-done.3, bf16[128,384]{1,0:T(8,128)(2,1)S(1)} %copy-done.2, ...), custom_call_target="tpu_custom_call" | custom-call | tf_op jit(solution)/shard_map/grads/pallas_call | solution.py:234
Async XLA Ops:
  0.6 33.2 %copy-start.4 = (bf16[256,256]{1,0:T(8,128)(2,1)S(1)}, bf16[256,256]{1,0:T(8,128)(2,1)}, u32[]{:S(2)}) copy-start(bf16[256,256]{1,0:T(8,128)(2,1)} %constant.13.clone.ib) | copy-start | bytes 393220
  0.6 33.2 %copy-start.6 = (bf16[128,128]{1,0:T(8,128)(2,1)S(1)}, bf16[128,128]{1,0:T(8,128)(2,1)}, u32[]{:S(2)}) copy-start(bf16[128,128]{1,0:T(8,128)(2,1)} %constant.10.clone.fa) | copy-start | bytes 98308
  0.7 33.2 %copy-start.7 = (bf16[64,128]{1,0:T(8,128)(2,1)S(1)}, bf16[64,128]{1,0:T(8,128)(2,1)}, u32[]{:S(2)}) copy-start(bf16[64,128]{1,0:T(8,128)(2,1)} %constant.14.clone.ia) | copy-start | bytes 49156
  2.1 31.8 %copy-start = (bf16[768,256]{1,0:T(8,128)(2,1)S(1)}, bf16[768,256]{1,0:T(8,128)(2,1)}, u32[]{:S(2)}) copy-start(bf16[768,256]{1,0:T(8,128)(2,1)} %constant.12.clone.fb) | copy-start | bytes 1179652
  2.1 31.8 %copy-start.5 = (f32[64,256]{1,0:T(8,128)S(1)}, f32[64,256]{1,0:T(8,128)}, u32[]{:S(2)}) copy-start(f32[64,256]{1,0:T(8,128)} %constant.11.clone.tw) | copy-start | bytes 196612
  60.1 10.5 %copy-start.1 = (bf16[128,384]{1,0:T(8,128)(2,1)S(1)}, bf16[128,384]{1,0:T(8,128)(2,1)}, u32[]{:S(2)}) copy-start(bf16[128,384]{1,0:T(8,128)(2,1)} %key_in.3) | copy-start | bytes 294916
  60.1 10.5 %copy-start.2 = (bf16[128,384]{1,0:T(8,128)(2,1)S(1)}, bf16[128,384]{1,0:T(8,128)(2,1)}, u32[]{:S(2)}) copy-start(bf16[128,384]{1,0:T(8,128)(2,1)} %value.3) | copy-start | bytes 294916
  60.2 10.5 %copy-start.3 = (bf16[128,384]{1,0:T(8,128)(2,1)S(1)}, bf16[128,384]{1,0:T(8,128)(2,1)}, u32[]{:S(2)}) copy-start(bf16[128,384]{1,0:T(8,128)(2,1)} %cot.1) | copy-start | bytes 294916

commit v5 on v4

--- a/solution.py
+++ b/solution.py
@@ -50,6 +50,11 @@
     return jnp.dot(left, right, preferred_element_type=F32)
 
 
+def mul_rows(left, right, step):
+    parts = [mul(left[i : i + step], right) for i in range(0, left.shape[0], step)]
+    return jnp.concatenate(parts, 0)
+
+
 def to_spectra(cols, fwd_a, twist, fwd_b):
     blocks, width = cols[0].shape
     data = jnp.concatenate(cols, 1)
@@ -61,14 +66,14 @@
         a_im = part[blocks:, s * width : (s + 1) * width]
         rows.append(jnp.concatenate([a_re * t_re - a_im * t_im, a_re * t_im + a_im * t_re], 1))
     high, low = split(jnp.concatenate(rows, 0))
-    return mul(jnp.concatenate([high, low, high], 1), fwd_b)
+    return mul_rows(jnp.concatenate([high, low, high], 1), fwd_b, 448)
 
 
 def from_spectra(spec, twist, inv_b, inv_a, scale):
     blocks = twist.shape[0]
     width = twist.shape[1] // 2
     count = spec.shape[0] // blocks
-    part = mul(spec.astype(BF16), inv_b)
+    part = mul_rows(spec.astype(BF16), inv_b, 448)
     t_re, t_im = twist[:, :width], twist[:, width:]
     cols = []
     for s in range(count):
@@ -192,7 +197,7 @@
     fils = filters // blocks
     per = (2 * repeat + 1) * fils
     scale = 1.0 / (length * math.sqrt(length))
-    first = blocks // 2 + 2
+    first = blocks // 2 + 3
     group = [(3 * groups // 4 + c) % groups for c in range(groups)]
     order = [(first + i) % blocks for i in range(blocks)]
     tables = [jnp.asarray(t) for t in make_tables(blocks, width, order)]

time: 72 us -> 71.1 us (0.987)
  no operation moved by 1% of the time
where the time goes in v5:
time: 71.1 us; the launch traced here: 70.5 us
  blocking collectives  66.2 us (93%)
  Pallas kernels  3.53 us (5%)
  between operations  0.72 us (1%)
    all_to_all x2, blocking collectives, swap(): lax.all_to_all(array.reshape(shape), 'seq', split_axis=0, concat_axis=0,...  55.9 us
    all_to_all x1, blocking collectives, local(): lax.all_to_all(taps, 'chan', split_axis=0, concat_axis=0, tiled=True, axi...  10.3 us

profile of v5, /device:TPU:6, one launch (start us, length us, event | category | flops | bytes accessed | tf_op | source)
XLA Modules:
  0.0 70.5 jit_solution(10658480018551823394)
XLA Ops:
  0.6 0.0 copy-start.4
  0.6 0.0 copy-start.6
  0.7 0.0 copy-start.7
  0.7 1.4 %gate.1 = bf16[896,128]{1,0:T(8,128)(2,1)S(1)} custom-call(bf16[128,384]{1,0:T(8,128)(2,1)} %query.1, bf16[128,384]{1,0:T(8,128)(2,1)} %key_in.3, bf16[128,384]{1,0:T(8,128)(2,1)} %value.3, bf16[128,384]{1,0:T(8,128)(2,1)} %cot.1, bf16[128,128]{1,0:T(8,128)(2,1)} %taps.2), custom_call_target="tpu_custom_call" | custom-call | tf_op jit(solution)/shard_map/gate/pallas_call | solution.py:214
  2.1 0.0 copy-start
  2.1 0.0 copy-start.5
  2.1 31.4 %all_to_all.21 = bf16[64,7,2,128]{3,2,1,0:T(2,128)(2,1)S(1)} all-to-all(bf16[64,7,2,128]{3,2,1,0:T(2,128)(2,1)S(1)} %bitcast.10), channel_id=1, replica_groups={{280,288,296,304,312,320,328,336,344,352,360,368,376,384,392,400,408,41..., dimensions={0} | all-to-all | bytes 458752 | tf_op jit(solution)/shard_map/all_to_all | solution.py:210
  33.5 0.0 copy-done.4
  33.5 0.0 copy-done.6
  33.5 0.0 copy-done.7
  33.5 0.0 copy-done
  33.5 0.0 copy-done.5
  33.5 1.2 %core.1 = bf16[896,128]{1,0:T(8,128)(2,1)S(1)} custom-call(bf16[896,128]{1,0:T(8,128)(2,1)S(1)} %bitcast.8, bf16[128,128]{1,0:T(8,128)(2,1)S(1)} %copy-done.6, f32[64,256]{1,0:T(8,128)S(1)} %copy-done.5, bf16[768,256]{1,0:T(8,128)(2,1)S(1)} %copy-done, bf16[256,256]{1,0:T(8,128)(2,1)S(1)} %copy-done.4, bf16[64,128]{1,0:T(8,128)(2,1)S(1)} %copy-done.7), custom_call_target="tpu_custom_call" | custom-call | tf_op jit(solution)/shard_map/core/pallas_call | solution.py:222
  34.7 24.4 %all_to_all.22 = bf16[64,7,2,128]{3,2,1,0:T(2,128)(2,1)S(1)} all-to-all(bf16[64,7,2,128]{3,2,1,0:T(2,128)(2,1)S(1)} %bitcast.9), channel_id=1, replica_groups={{280,288,296,304,312,320,328,336,344,352,360,368,376,384,392,400,408,41..., dimensions={0} | all-to-all | bytes 458752 | tf_op jit(solution)/shard_map/all_to_all | solution.py:210
  59.2 0.0 copy-start.1
  59.2 0.0 copy-start.2
  59.2 0.0 copy-start.3
  59.2 0.1 taps.3
  59.3 10.3 %all_to_all.23 = bf16[8,16,128]{2,1,0:T(8,128)(2,1)S(1)} all-to-all(bf16[8,16,128]{2,1,0:T(8,128)(2,1)S(1)} %bitcast.12), channel_id=1, replica_groups={{6,7,0,1,2,3,4,5},{14,15,8,9,10,11,12,13},{22,23,16,17,18,19,20,21},{30..., dimensions={0} | all-to-all | bytes 65536 | tf_op jit(solution)/shard_map/all_to_all | solution.py:238
  69.6 0.0 copy-done.1
  69.6 0.0 copy-done.2
  69.6 0.0 copy-done.3
  69.6 0.9 %grads.1 = (bf16[128,384]{1,0:T(8,128)(2,1)}, bf16[128,384]{1,0:T(8,128)(2,1)}, bf16[128,384]{1,0:T(8,128)(2,1)}, f32[16,128]{1,0:T(8,128)}) custom-call(bf16[896,128]{1,0:T(8,128)(2,1)S(1)} %bitcast.7, bf16[128,128]{1,0:T(8,128)(2,1)S(1)} %bitcast.11, bf16[128,384]{1,0:T(8,128)(2,1)S(1)} %copy-done.3, bf16[128,384]{1,0:T(8,128)(2,1)S(1)} %copy-done.2, ...), custom_call_target="tpu_custom_call" | custom-call | tf_op jit(solution)/shard_map/grads/pallas_call | solution.py:239
Async XLA Ops:
  0.6 32.9 %copy-start.4 = (bf16[256,256]{1,0:T(8,128)(2,1)S(1)}, bf16[256,256]{1,0:T(8,128)(2,1)}, u32[]{:S(2)}) copy-start(bf16[256,256]{1,0:T(8,128)(2,1)} %constant.13.clone.ib) | copy-start | bytes 393220
  0.6 32.9 %copy-start.6 = (bf16[128,128]{1,0:T(8,128)(2,1)S(1)}, bf16[128,128]{1,0:T(8,128)(2,1)}, u32[]{:S(2)}) copy-start(bf16[128,128]{1,0:T(8,128)(2,1)} %constant.10.clone.fa) | copy-start | bytes 98308
  0.7 32.9 %copy-start.7 = (bf16[64,128]{1,0:T(8,128)(2,1)S(1)}, bf16[64,128]{1,0:T(8,128)(2,1)}, u32[]{:S(2)}) copy-start(bf16[64,128]{1,0:T(8,128)(2,1)} %constant.14.clone.ia) | copy-start | bytes 49156
  2.1 31.5 %copy-start = (bf16[768,256]{1,0:T(8,128)(2,1)S(1)}, bf16[768,256]{1,0:T(8,128)(2,1)}, u32[]{:S(2)}) copy-start(bf16[768,256]{1,0:T(8,128)(2,1)} %constant.12.clone.fb) | copy-start | bytes 1179652
  2.1 31.5 %copy-start.5 = (f32[64,256]{1,0:T(8,128)S(1)}, f32[64,256]{1,0:T(8,128)}, u32[]{:S(2)}) copy-start(f32[64,256]{1,0:T(8,128)} %constant.11.clone.tw) | copy-start | bytes 196612
  59.2 10.5 %copy-start.1 = (bf16[128,384]{1,0:T(8,128)(2,1)S(1)}, bf16[128,384]{1,0:T(8,128)(2,1)}, u32[]{:S(2)}) copy-start(bf16[128,384]{1,0:T(8,128)(2,1)} %key_in.3) | copy-start | bytes 294916
  59.2 10.5 %copy-start.2 = (bf16[128,384]{1,0:T(8,128)(2,1)S(1)}, bf16[128,384]{1,0:T(8,128)(2,1)}, u32[]{:S(2)}) copy-start(bf16[128,384]{1,0:T(8,128)(2,1)} %value.3) | copy-start | bytes 294916
  59.2 10.5 %copy-start.3 = (bf16[128,384]{1,0:T(8,128)(2,1)S(1)}, bf16[128,384]{1,0:T(8,128)(2,1)}, u32[]{:S(2)}) copy-start(bf16[128,384]{1,0:T(8,128)(2,1)} %cot.1) | copy-start | bytes 294916

commit v6 on v5

--- a/solution.py
+++ b/solution.py
@@ -199,7 +199,7 @@
     scale = 1.0 / (length * math.sqrt(length))
     first = blocks // 2 + 3
     group = [(3 * groups // 4 + c) % groups for c in range(groups)]
-    order = [(first + i) % blocks for i in range(blocks)]
+    order = [(first - i) % blocks for i in range(blocks)]
     tables = [jnp.asarray(t) for t in make_tables(blocks, width, order)]
     params = pltpu.CompilerParams(vmem_limit_bytes=VMEM_LIMIT)
     packed = jax.ShapeDtypeStruct((blocks * per, width), BF16)

time: 71.1 us -> 70.8 us (level)
  no operation moved by 1% of the time
where the time goes in v6:
time: 70.8 us; the launch traced here: 70 us
  blocking collectives  65.7 us (93%)
  Pallas kernels  3.53 us (5%)
  between operations  0.72 us (1%)
    all_to_all x2, blocking collectives, swap(): lax.all_to_all(array.reshape(shape), 'seq', split_axis=0, concat_axis=0,...  55.4 us
    all_to_all x1, blocking collectives, local(): lax.all_to_all(taps, 'chan', split_axis=0, concat_axis=0, tiled=True, axi...  10.3 us

profile of v6, /device:TPU:6, one launch (start us, length us, event | category | flops | bytes accessed | tf_op | source)
XLA Modules:
  0.0 70.0 jit_solution(10151823090225526359)
XLA Ops:
  0.6 0.0 copy-start.4
  0.6 0.0 copy-start.6
  0.7 0.0 copy-start.7
  0.7 1.4 %gate.1 = bf16[896,128]{1,0:T(8,128)(2,1)S(1)} custom-call(bf16[128,384]{1,0:T(8,128)(2,1)} %query.1, bf16[128,384]{1,0:T(8,128)(2,1)} %key_in.3, bf16[128,384]{1,0:T(8,128)(2,1)} %value.3, bf16[128,384]{1,0:T(8,128)(2,1)} %cot.1, bf16[128,128]{1,0:T(8,128)(2,1)} %taps.2), custom_call_target="tpu_custom_call" | custom-call | tf_op jit(solution)/shard_map/gate/pallas_call | solution.py:214
  2.1 0.0 copy-start
  2.1 0.0 copy-start.5
  2.1 31.1 %all_to_all.21 = bf16[64,7,2,128]{3,2,1,0:T(2,128)(2,1)S(1)} all-to-all(bf16[64,7,2,128]{3,2,1,0:T(2,128)(2,1)S(1)} %bitcast.10), channel_id=1, replica_groups={{280,272,264,256,248,240,232,224,216,208,200,192,184,176,168,160,152,14..., dimensions={0} | all-to-all | bytes 458752 | tf_op jit(solution)/shard_map/all_to_all | solution.py:210
  33.2 0.0 copy-done.4
  33.2 0.0 copy-done.6
  33.2 0.0 copy-done.7
  33.2 0.0 copy-done
  33.2 0.0 copy-done.5
  33.2 1.2 %core.1 = bf16[896,128]{1,0:T(8,128)(2,1)S(1)} custom-call(bf16[896,128]{1,0:T(8,128)(2,1)S(1)} %bitcast.8, bf16[128,128]{1,0:T(8,128)(2,1)S(1)} %copy-done.6, f32[64,256]{1,0:T(8,128)S(1)} %copy-done.5, bf16[768,256]{1,0:T(8,128)(2,1)S(1)} %copy-done, bf16[256,256]{1,0:T(8,128)(2,1)S(1)} %copy-done.4, bf16[64,128]{1,0:T(8,128)(2,1)S(1)} %copy-done.7), custom_call_target="tpu_custom_call" | custom-call | tf_op jit(solution)/shard_map/core/pallas_call | solution.py:222
  34.4 24.3 %all_to_all.22 = bf16[64,7,2,128]{3,2,1,0:T(2,128)(2,1)S(1)} all-to-all(bf16[64,7,2,128]{3,2,1,0:T(2,128)(2,1)S(1)} %bitcast.9), channel_id=1, replica_groups={{280,272,264,256,248,240,232,224,216,208,200,192,184,176,168,160,152,14..., dimensions={0} | all-to-all | bytes 458752 | tf_op jit(solution)/shard_map/all_to_all | solution.py:210
  58.7 0.0 copy-start.1
  58.7 0.0 copy-start.2
  58.7 0.0 copy-start.3
  58.7 0.1 taps.3
  58.8 10.3 %all_to_all.23 = bf16[8,16,128]{2,1,0:T(8,128)(2,1)S(1)} all-to-all(bf16[8,16,128]{2,1,0:T(8,128)(2,1)S(1)} %bitcast.12), channel_id=1, replica_groups={{6,7,0,1,2,3,4,5},{14,15,8,9,10,11,12,13},{22,23,16,17,18,19,20,21},{30..., dimensions={0} | all-to-all | bytes 65536 | tf_op jit(solution)/shard_map/all_to_all | solution.py:238
  69.1 0.0 copy-done.1
  69.1 0.0 copy-done.2
  69.1 0.0 copy-done.3
  69.1 0.9 %grads.1 = (bf16[128,384]{1,0:T(8,128)(2,1)}, bf16[128,384]{1,0:T(8,128)(2,1)}, bf16[128,384]{1,0:T(8,128)(2,1)}, f32[16,128]{1,0:T(8,128)}) custom-call(bf16[896,128]{1,0:T(8,128)(2,1)S(1)} %bitcast.7, bf16[128,128]{1,0:T(8,128)(2,1)S(1)} %bitcast.11, bf16[128,384]{1,0:T(8,128)(2,1)S(1)} %copy-done.3, bf16[128,384]{1,0:T(8,128)(2,1)S(1)} %copy-done.2, ...), custom_call_target="tpu_custom_call" | custom-call | tf_op jit(solution)/shard_map/grads/pallas_call | solution.py:239
Async XLA Ops:
  0.6 32.5 %copy-start.4 = (bf16[256,256]{1,0:T(8,128)(2,1)S(1)}, bf16[256,256]{1,0:T(8,128)(2,1)}, u32[]{:S(2)}) copy-start(bf16[256,256]{1,0:T(8,128)(2,1)} %constant.13.clone.ib) | copy-start | bytes 393220
  0.6 32.5 %copy-start.6 = (bf16[128,128]{1,0:T(8,128)(2,1)S(1)}, bf16[128,128]{1,0:T(8,128)(2,1)}, u32[]{:S(2)}) copy-start(bf16[128,128]{1,0:T(8,128)(2,1)} %constant.10.clone.fa) | copy-start | bytes 98308
  0.7 32.5 %copy-start.7 = (bf16[64,128]{1,0:T(8,128)(2,1)S(1)}, bf16[64,128]{1,0:T(8,128)(2,1)}, u32[]{:S(2)}) copy-start(bf16[64,128]{1,0:T(8,128)(2,1)} %constant.14.clone.ia) | copy-start | bytes 49156
  2.1 31.1 %copy-start = (bf16[768,256]{1,0:T(8,128)(2,1)S(1)}, bf16[768,256]{1,0:T(8,128)(2,1)}, u32[]{:S(2)}) copy-start(bf16[768,256]{1,0:T(8,128)(2,1)} %constant.12.clone.fb) | copy-start | bytes 1179652
  2.1 31.1 %copy-start.5 = (f32[64,256]{1,0:T(8,128)S(1)}, f32[64,256]{1,0:T(8,128)}, u32[]{:S(2)}) copy-start(f32[64,256]{1,0:T(8,128)} %constant.11.clone.tw) | copy-start | bytes 196612
  58.7 10.5 %copy-start.1 = (bf16[128,384]{1,0:T(8,128)(2,1)S(1)}, bf16[128,384]{1,0:T(8,128)(2,1)}, u32[]{:S(2)}) copy-start(bf16[128,384]{1,0:T(8,128)(2,1)} %key_in.3) | copy-start | bytes 294916
  58.7 10.5 %copy-start.2 = (bf16[128,384]{1,0:T(8,128)(2,1)S(1)}, bf16[128,384]{1,0:T(8,128)(2,1)}, u32[]{:S(2)}) copy-start(bf16[128,384]{1,0:T(8,128)(2,1)} %value.3) | copy-start | bytes 294916
  58.7 10.5 %copy-start.3 = (bf16[128,384]{1,0:T(8,128)(2,1)S(1)}, bf16[128,384]{1,0:T(8,128)(2,1)}, u32[]{:S(2)}) copy-start(bf16[128,384]{1,0:T(8,128)(2,1)} %cot.1) | copy-start | bytes 294916

commit v7 on v6

--- a/solution.py
+++ b/solution.py
@@ -113,11 +113,11 @@
     copies[3].wait()
     copies[4].wait()
     put_product(repeat * fils, g_in, q_in)
-    out_ref[...] = hold[...].astype(BF16)
+    out_ref[...] = hold[: out_ref.shape[0]].astype(BF16)
 
 
 def take_columns(ref, hold, per, blocks):
-    hold[...] = ref[...].astype(F32)
+    hold[: ref.shape[0]] = ref[...].astype(F32)
     return [hold[pl.ds(s, blocks, stride=per), :].astype(BF16) for s in range(per)]
 
 
@@ -149,7 +149,7 @@
     result = from_spectra(jnp.concatenate(prods, 0), tw[...], ib[...], ia[...], scale)
     for s in range(per):
         hold[pl.ds(s, blocks, stride=per), :] = result[:, s * width : (s + 1) * width]
-    out_ref[...] = hold[...].astype(BF16)
+    out_ref[...] = hold[: out_ref.shape[0]].astype(BF16)
 
 
 def back_rows(rows, first, blocks, width):
@@ -160,7 +160,7 @@
 
 def taps_kernel(repeat, blocks, group, rows_ref, taps, hold):
     width = taps.shape[1]
-    hold[...] = rows_ref[...].astype(F32)
+    hold[: rows_ref.shape[0]] = rows_ref[...].astype(F32)
     flipped = back_rows(hold, 2 * repeat * (width // blocks), blocks, width).astype(BF16)
     lags = width // len(group)
     for c, owner in enumerate(group):
@@ -172,7 +172,7 @@
 ):
     width = cot.shape[0]
     fils = width // blocks
-    hold[...] = rows_ref[...].astype(F32)
+    hold[: rows_ref.shape[0]] = rows_ref[...].astype(F32)
     lags = grad_filter.shape[0]
     total = part_ref[:lags].astype(F32)
     for c in range(1, width // lags):
@@ -203,7 +203,7 @@
     tables = [jnp.asarray(t) for t in make_tables(blocks, width, order)]
     params = pltpu.CompilerParams(vmem_limit_bytes=VMEM_LIMIT)
     packed = jax.ShapeDtypeStruct((blocks * per, width), BF16)
-    hold = pltpu.VMEM((blocks * per, width), F32)
+    hold = pltpu.VMEM((blocks * per + 16, width), F32)
 
     def swap(array):
         shape = (blocks, per // fils, fils, width)

time: 70.8 us -> 70.8 us (level)
  no operation moved by 1% of the time
where the time goes in v7:
time: 70.8 us; the launch traced here: 70 us
  blocking collectives  65.7 us (93%)
  Pallas kernels  3.53 us (5%)
  between operations  0.72 us (1%)
    all_to_all x2, blocking collectives, swap(): lax.all_to_all(array.reshape(shape), 'seq', split_axis=0, concat_axis=0,...  55.4 us
    all_to_all x1, blocking collectives, local(): lax.all_to_all(taps, 'chan', split_axis=0, concat_axis=0, tiled=True, axi...  10.3 us

profile of v7, /device:TPU:6, one launch (start us, length us, event | category | flops | bytes accessed | tf_op | source)
XLA Modules:
  0.0 70.0 jit_solution(2650673105837971580)
XLA Ops:
  0.6 0.0 copy-start.4
  0.6 0.0 copy-start.6
  0.7 0.0 copy-start.7
  0.7 1.4 %gate.1 = bf16[896,128]{1,0:T(8,128)(2,1)S(1)} custom-call(bf16[128,384]{1,0:T(8,128)(2,1)} %query.1, bf16[128,384]{1,0:T(8,128)(2,1)} %key_in.3, bf16[128,384]{1,0:T(8,128)(2,1)} %value.3, bf16[128,384]{1,0:T(8,128)(2,1)} %cot.1, bf16[128,128]{1,0:T(8,128)(2,1)} %taps.2), custom_call_target="tpu_custom_call" | custom-call | tf_op jit(solution)/shard_map/gate/pallas_call | solution.py:214
  2.1 0.0 copy-start
  2.1 0.0 copy-start.5
  2.1 31.1 %all_to_all.21 = bf16[64,7,2,128]{3,2,1,0:T(2,128)(2,1)S(1)} all-to-all(bf16[64,7,2,128]{3,2,1,0:T(2,128)(2,1)S(1)} %bitcast.10), channel_id=1, replica_groups={{280,272,264,256,248,240,232,224,216,208,200,192,184,176,168,160,152,14..., dimensions={0} | all-to-all | bytes 458752 | tf_op jit(solution)/shard_map/all_to_all | solution.py:210
  33.2 0.0 copy-done.4
  33.2 0.0 copy-done.6
  33.2 0.0 copy-done.7
  33.2 0.0 copy-done
  33.2 0.0 copy-done.5
  33.2 1.2 %core.1 = bf16[896,128]{1,0:T(8,128)(2,1)S(1)} custom-call(bf16[896,128]{1,0:T(8,128)(2,1)S(1)} %bitcast.8, bf16[128,128]{1,0:T(8,128)(2,1)S(1)} %copy-done.6, f32[64,256]{1,0:T(8,128)S(1)} %copy-done.5, bf16[768,256]{1,0:T(8,128)(2,1)S(1)} %copy-done, bf16[256,256]{1,0:T(8,128)(2,1)S(1)} %copy-done.4, bf16[64,128]{1,0:T(8,128)(2,1)S(1)} %copy-done.7), custom_call_target="tpu_custom_call" | custom-call | tf_op jit(solution)/shard_map/core/pallas_call | solution.py:222
  34.4 24.3 %all_to_all.22 = bf16[64,7,2,128]{3,2,1,0:T(2,128)(2,1)S(1)} all-to-all(bf16[64,7,2,128]{3,2,1,0:T(2,128)(2,1)S(1)} %bitcast.9), channel_id=1, replica_groups={{280,272,264,256,248,240,232,224,216,208,200,192,184,176,168,160,152,14..., dimensions={0} | all-to-all | bytes 458752 | tf_op jit(solution)/shard_map/all_to_all | solution.py:210
  58.7 0.0 copy-start.1
  58.7 0.0 copy-start.2
  58.7 0.0 copy-start.3
  58.7 0.1 taps.3
  58.8 10.3 %all_to_all.23 = bf16[8,16,128]{2,1,0:T(8,128)(2,1)S(1)} all-to-all(bf16[8,16,128]{2,1,0:T(8,128)(2,1)S(1)} %bitcast.12), channel_id=1, replica_groups={{6,7,0,1,2,3,4,5},{14,15,8,9,10,11,12,13},{22,23,16,17,18,19,20,21},{30..., dimensions={0} | all-to-all | bytes 65536 | tf_op jit(solution)/shard_map/all_to_all | solution.py:238
  69.1 0.0 copy-done.1
  69.1 0.0 copy-done.2
  69.1 0.0 copy-done.3
  69.1 0.9 %grads.1 = (bf16[128,384]{1,0:T(8,128)(2,1)}, bf16[128,384]{1,0:T(8,128)(2,1)}, bf16[128,384]{1,0:T(8,128)(2,1)}, f32[16,128]{1,0:T(8,128)}) custom-call(bf16[896,128]{1,0:T(8,128)(2,1)S(1)} %bitcast.7, bf16[128,128]{1,0:T(8,128)(2,1)S(1)} %bitcast.11, bf16[128,384]{1,0:T(8,128)(2,1)S(1)} %copy-done.3, bf16[128,384]{1,0:T(8,128)(2,1)S(1)} %copy-done.2, ...), custom_call_target="tpu_custom_call" | custom-call | tf_op jit(solution)/shard_map/grads/pallas_call | solution.py:239
Async XLA Ops:
  0.6 32.5 %copy-start.4 = (bf16[256,256]{1,0:T(8,128)(2,1)S(1)}, bf16[256,256]{1,0:T(8,128)(2,1)}, u32[]{:S(2)}) copy-start(bf16[256,256]{1,0:T(8,128)(2,1)} %constant.13.clone.ib) | copy-start | bytes 393220
  0.6 32.5 %copy-start.6 = (bf16[128,128]{1,0:T(8,128)(2,1)S(1)}, bf16[128,128]{1,0:T(8,128)(2,1)}, u32[]{:S(2)}) copy-start(bf16[128,128]{1,0:T(8,128)(2,1)} %constant.10.clone.fa) | copy-start | bytes 98308
  0.7 32.5 %copy-start.7 = (bf16[64,128]{1,0:T(8,128)(2,1)S(1)}, bf16[64,128]{1,0:T(8,128)(2,1)}, u32[]{:S(2)}) copy-start(bf16[64,128]{1,0:T(8,128)(2,1)} %constant.14.clone.ia) | copy-start | bytes 49156
  2.1 31.1 %copy-start = (bf16[768,256]{1,0:T(8,128)(2,1)S(1)}, bf16[768,256]{1,0:T(8,128)(2,1)}, u32[]{:S(2)}) copy-start(bf16[768,256]{1,0:T(8,128)(2,1)} %constant.12.clone.fb) | copy-start | bytes 1179652
  2.1 31.1 %copy-start.5 = (f32[64,256]{1,0:T(8,128)S(1)}, f32[64,256]{1,0:T(8,128)}, u32[]{:S(2)}) copy-start(f32[64,256]{1,0:T(8,128)} %constant.11.clone.tw) | copy-start | bytes 196612
  58.7 10.5 %copy-start.1 = (bf16[128,384]{1,0:T(8,128)(2,1)S(1)}, bf16[128,384]{1,0:T(8,128)(2,1)}, u32[]{:S(2)}) copy-start(bf16[128,384]{1,0:T(8,128)(2,1)} %key_in.3) | copy-start | bytes 294916
  58.7 10.5 %copy-start.2 = (bf16[128,384]{1,0:T(8,128)(2,1)S(1)}, bf16[128,384]{1,0:T(8,128)(2,1)}, u32[]{:S(2)}) copy-start(bf16[128,384]{1,0:T(8,128)(2,1)} %value.3) | copy-start | bytes 294916
  58.7 10.5 %copy-start.3 = (bf16[128,384]{1,0:T(8,128)(2,1)S(1)}, bf16[128,384]{1,0:T(8,128)(2,1)}, u32[]{:S(2)}) copy-start(bf16[128,384]{1,0:T(8,128)(2,1)} %cot.1) | copy-start | bytes 294916

commit v8 on v7

--- a/solution.py
+++ b/solution.py
@@ -168,23 +168,38 @@
 
 
 def grads_kernel(
-    repeat, blocks, rows_ref, part_ref, cot, value, key_in, grad_query, grad_key, grad_value, grad_filter, hold
+    repeat, blocks, rows_ref, part_ref, cot, value, key_in, out_query, out_key, out_value, out_filter, hold, *scratch
 ):
+    grad_query, grad_key, grad_value, grad_filter, sems = scratch
     width = cot.shape[0]
     fils = width // blocks
-    hold[: rows_ref.shape[0]] = rows_ref[...].astype(F32)
+    copies = [
+        pltpu.make_async_copy(source, target, sems.at[i])
+        for i, (source, target) in enumerate(
+            ((grad_query, out_query), (grad_key, out_key), (grad_value, out_value), (grad_filter, out_filter))
+        )
+    ]
     lags = grad_filter.shape[0]
     total = part_ref[:lags].astype(F32)
     for c in range(1, width // lags):
         total = total + part_ref[c * lags : (c + 1) * lags].astype(F32)
     grad_filter[...] = total
+    copies[3].start()
+    hold[: rows_ref.shape[0]] = rows_ref[...].astype(F32)
     for c in range(repeat):
         at = slice(c * width, (c + 1) * width)
         conv = back_rows(hold, c * fils, blocks, width)
         grad_query[:, at] = (cot[:, at].astype(F32) * conv).astype(BF16)
+    copies[0].start()
+    for c in range(repeat):
+        at = slice(c * width, (c + 1) * width)
         back = back_rows(hold, (repeat + c) * fils, blocks, width)
         grad_key[:, at] = (back * value[:, at].astype(F32)).astype(BF16)
         grad_value[:, at] = (back * key_in[:, at].astype(F32)).astype(BF16)
+    copies[1].start()
+    copies[2].start()
+    for copy in copies:
+        copy.wait()
 
 
 def local(query, key_in, value, cotangent, filter_raw):
@@ -199,7 +214,8 @@
     scale = 1.0 / (length * math.sqrt(length))
     first = blocks // 2 + 3
     group = [(3 * groups // 4 + c) % groups for c in range(groups)]
-    order = [(first - i) % blocks for i in range(blocks)]
+    bits = blocks.bit_length() - 1
+    order = [(first - int(format(i, "0%db" % bits)[::-1], 2)) % blocks for i in range(blocks)]
     tables = [jnp.asarray(t) for t in make_tables(blocks, width, order)]
     params = pltpu.CompilerParams(vmem_limit_bytes=VMEM_LIMIT)
     packed = jax.ShapeDtypeStruct((blocks * per, width), BF16)
@@ -239,7 +255,8 @@
     return pl.pallas_call(
         functools.partial(grads_kernel, repeat, blocks),
         out_shape=(like, like, like, jax.ShapeDtypeStruct((width // groups, filters), F32)),
-        scratch_shapes=[hold],
+        out_specs=[pl.BlockSpec(memory_space=pl.ANY)] * 4,
+        scratch_shapes=[hold, wide, wide, wide, pltpu.VMEM((width // groups, filters), F32), pltpu.SemaphoreType.DMA((4,))],
         compiler_params=params,
         name="grads",
     )(rows, taps, cotangent, value, key_in)

time: 70.8 us -> 70.6 us (level)
  no operation moved by 1% of the time
where the time goes in v8:
time: 70.6 us; the launch traced here: 70 us
  blocking collectives  65.7 us (93%)
  Pallas kernels  3.56 us (5%)
  between operations  0.72 us (1%)
    all_to_all x2, blocking collectives, swap(): lax.all_to_all(array.reshape(shape), 'seq', split_axis=0, concat_axis=0,...  55.4 us
    all_to_all x1, blocking collectives, local(): lax.all_to_all(taps, 'chan', split_axis=0, concat_axis=0, tiled=True, axi...  10.3 us

profile of v8, /device:TPU:6, one launch (start us, length us, event | category | flops | bytes accessed | tf_op | source)
XLA Modules:
  0.0 70.0 jit_solution(2255482904737339181)
XLA Ops:
  0.6 0.0 copy-start.4
  0.6 0.0 copy-start.6
  0.7 0.0 copy-start.7
  0.7 1.4 %gate.1 = bf16[896,128]{1,0:T(8,128)(2,1)S(1)} custom-call(bf16[128,384]{1,0:T(8,128)(2,1)} %query.1, bf16[128,384]{1,0:T(8,128)(2,1)} %key_in.3, bf16[128,384]{1,0:T(8,128)(2,1)} %value.3, bf16[128,384]{1,0:T(8,128)(2,1)} %cot.1, bf16[128,128]{1,0:T(8,128)(2,1)} %taps.2), custom_call_target="tpu_custom_call" | custom-call | tf_op jit(solution)/shard_map/gate/pallas_call | solution.py:230
  2.1 0.0 copy-start
  2.1 0.0 copy-start.5
  2.1 31.1 %all_to_all.21 = bf16[64,7,2,128]{3,2,1,0:T(2,128)(2,1)S(1)} all-to-all(bf16[64,7,2,128]{3,2,1,0:T(2,128)(2,1)S(1)} %bitcast.10), channel_id=1, replica_groups={{280,24,152,408,216,472,88,344,248,504,120,376,184,440,56,312,264,8,136..., dimensions={0} | all-to-all | bytes 458752 | tf_op jit(solution)/shard_map/all_to_all | solution.py:226
  33.2 0.0 copy-done.4
  33.2 0.0 copy-done.6
  33.2 0.0 copy-done.7
  33.2 0.0 copy-done
  33.3 0.0 copy-done.5
  33.3 1.2 %core.1 = bf16[896,128]{1,0:T(8,128)(2,1)S(1)} custom-call(bf16[896,128]{1,0:T(8,128)(2,1)S(1)} %bitcast.8, bf16[128,128]{1,0:T(8,128)(2,1)S(1)} %copy-done.6, f32[64,256]{1,0:T(8,128)S(1)} %copy-done.5, bf16[768,256]{1,0:T(8,128)(2,1)S(1)} %copy-done, bf16[256,256]{1,0:T(8,128)(2,1)S(1)} %copy-done.4, bf16[64,128]{1,0:T(8,128)(2,1)S(1)} %copy-done.7), custom_call_target="tpu_custom_call" | custom-call | tf_op jit(solution)/shard_map/core/pallas_call | solution.py:238
  34.4 24.2 %all_to_all.22 = bf16[64,7,2,128]{3,2,1,0:T(2,128)(2,1)S(1)} all-to-all(bf16[64,7,2,128]{3,2,1,0:T(2,128)(2,1)S(1)} %bitcast.9), channel_id=1, replica_groups={{280,24,152,408,216,472,88,344,248,504,120,376,184,440,56,312,264,8,136..., dimensions={0} | all-to-all | bytes 458752 | tf_op jit(solution)/shard_map/all_to_all | solution.py:226
  58.6 0.0 copy-start.1
  58.6 0.0 copy-start.2
  58.6 0.0 copy-start.3
  58.6 0.1 taps.3
  58.8 10.3 %all_to_all.23 = bf16[8,16,128]{2,1,0:T(8,128)(2,1)S(1)} all-to-all(bf16[8,16,128]{2,1,0:T(8,128)(2,1)S(1)} %bitcast.12), channel_id=1, replica_groups={{6,7,0,1,2,3,4,5},{14,15,8,9,10,11,12,13},{22,23,16,17,18,19,20,21},{30..., dimensions={0} | all-to-all | bytes 65536 | tf_op jit(solution)/shard_map/all_to_all | solution.py:254
  69.1 0.0 copy-done.1
  69.1 0.0 copy-done.2
  69.1 0.0 copy-done.3
  69.1 0.9 %grads.1 = (bf16[128,384]{1,0:T(8,128)(2,1)}, bf16[128,384]{1,0:T(8,128)(2,1)}, bf16[128,384]{1,0:T(8,128)(2,1)}, f32[16,128]{1,0:T(8,128)}) custom-call(bf16[896,128]{1,0:T(8,128)(2,1)S(1)} %bitcast.7, bf16[128,128]{1,0:T(8,128)(2,1)S(1)} %bitcast.11, bf16[128,384]{1,0:T(8,128)(2,1)S(1)} %copy-done.3, bf16[128,384]{1,0:T(8,128)(2,1)S(1)} %copy-done.2, ...), custom_call_target="tpu_custom_call" | custom-call | tf_op jit(solution)/shard_map/grads/pallas_call | solution.py:255
Async XLA Ops:
  0.6 32.6 %copy-start.4 = (bf16[256,256]{1,0:T(8,128)(2,1)S(1)}, bf16[256,256]{1,0:T(8,128)(2,1)}, u32[]{:S(2)}) copy-start(bf16[256,256]{1,0:T(8,128)(2,1)} %constant.13.clone.ib) | copy-start | bytes 393220
  0.6 32.6 %copy-start.6 = (bf16[128,128]{1,0:T(8,128)(2,1)S(1)}, bf16[128,128]{1,0:T(8,128)(2,1)}, u32[]{:S(2)}) copy-start(bf16[128,128]{1,0:T(8,128)(2,1)} %constant.10.clone.fa) | copy-start | bytes 98308
  0.7 32.6 %copy-start.7 = (bf16[64,128]{1,0:T(8,128)(2,1)S(1)}, bf16[64,128]{1,0:T(8,128)(2,1)}, u32[]{:S(2)}) copy-start(bf16[64,128]{1,0:T(8,128)(2,1)} %constant.14.clone.ia) | copy-start | bytes 49156
  2.1 31.2 %copy-start = (bf16[768,256]{1,0:T(8,128)(2,1)S(1)}, bf16[768,256]{1,0:T(8,128)(2,1)}, u32[]{:S(2)}) copy-start(bf16[768,256]{1,0:T(8,128)(2,1)} %constant.12.clone.fb) | copy-start | bytes 1179652
  2.1 31.2 %copy-start.5 = (f32[64,256]{1,0:T(8,128)S(1)}, f32[64,256]{1,0:T(8,128)}, u32[]{:S(2)}) copy-start(f32[64,256]{1,0:T(8,128)} %constant.11.clone.tw) | copy-start | bytes 196612
  58.6 10.5 %copy-start.1 = (bf16[128,384]{1,0:T(8,128)(2,1)S(1)}, bf16[128,384]{1,0:T(8,128)(2,1)}, u32[]{:S(2)}) copy-start(bf16[128,384]{1,0:T(8,128)(2,1)} %key_in.3) | copy-start | bytes 294916
  58.6 10.5 %copy-start.2 = (bf16[128,384]{1,0:T(8,128)(2,1)S(1)}, bf16[128,384]{1,0:T(8,128)(2,1)}, u32[]{:S(2)}) copy-start(bf16[128,384]{1,0:T(8,128)(2,1)} %value.3) | copy-start | bytes 294916
  58.6 10.5 %copy-start.3 = (bf16[128,384]{1,0:T(8,128)(2,1)S(1)}, bf16[128,384]{1,0:T(8,128)(2,1)}, u32[]{:S(2)}) copy-start(bf16[128,384]{1,0:T(8,128)(2,1)} %cot.1) | copy-start | bytes 294916

commit v9 on v8

--- a/solution.py
+++ b/solution.py
@@ -214,8 +214,7 @@
     scale = 1.0 / (length * math.sqrt(length))
     first = blocks // 2 + 3
     group = [(3 * groups // 4 + c) % groups for c in range(groups)]
-    bits = blocks.bit_length() - 1
-    order = [(first - int(format(i, "0%db" % bits)[::-1], 2)) % blocks for i in range(blocks)]
+    order = [(first - i) % blocks for i in range(blocks)]
     tables = [jnp.asarray(t) for t in make_tables(blocks, width, order)]
     params = pltpu.CompilerParams(vmem_limit_bytes=VMEM_LIMIT)
     packed = jax.ShapeDtypeStruct((blocks * per, width), BF16)

time: 70.6 us -> 70.9 us (level)
  no operation moved by 1% of the time
where the time goes in v9:
time: 70.9 us; the launch traced here: 70.1 us
  blocking collectives  65.7 us (93%)
  Pallas kernels  3.56 us (5%)
  between operations  0.72 us (1%)
    all_to_all x2, blocking collectives, swap(): lax.all_to_all(array.reshape(shape), 'seq', split_axis=0, concat_axis=0,...  55.4 us
    all_to_all x1, blocking collectives, local(): lax.all_to_all(taps, 'chan', split_axis=0, concat_axis=0, tiled=True, axi...  10.3 us

profile of v9, /device:TPU:6, one launch (start us, length us, event | category | flops | bytes accessed | tf_op | source)
XLA Modules:
  0.0 70.1 jit_solution(4274240315138662020)
XLA Ops:
  0.6 0.0 copy-start.4
  0.6 0.0 copy-start.6
  0.7 0.0 copy-start.7
  0.7 1.4 %gate.1 = bf16[896,128]{1,0:T(8,128)(2,1)S(1)} custom-call(bf16[128,384]{1,0:T(8,128)(2,1)} %query.1, bf16[128,384]{1,0:T(8,128)(2,1)} %key_in.3, bf16[128,384]{1,0:T(8,128)(2,1)} %value.3, bf16[128,384]{1,0:T(8,128)(2,1)} %cot.1, bf16[128,128]{1,0:T(8,128)(2,1)} %taps.2), custom_call_target="tpu_custom_call" | custom-call | tf_op jit(solution)/shard_map/gate/pallas_call | solution.py:229
  2.1 0.0 copy-start
  2.1 0.0 copy-start.5
  2.1 31.1 %all_to_all.21 = bf16[64,7,2,128]{3,2,1,0:T(2,128)(2,1)S(1)} all-to-all(bf16[64,7,2,128]{3,2,1,0:T(2,128)(2,1)S(1)} %bitcast.10), channel_id=1, replica_groups={{280,272,264,256,248,240,232,224,216,208,200,192,184,176,168,160,152,14..., dimensions={0} | all-to-all | bytes 458752 | tf_op jit(solution)/shard_map/all_to_all | solution.py:225
  33.2 0.0 copy-done.4
  33.2 0.0 copy-done.6
  33.2 0.0 copy-done.7
  33.2 0.0 copy-done
  33.2 0.0 copy-done.5
  33.2 1.2 %core.1 = bf16[896,128]{1,0:T(8,128)(2,1)S(1)} custom-call(bf16[896,128]{1,0:T(8,128)(2,1)S(1)} %bitcast.8, bf16[128,128]{1,0:T(8,128)(2,1)S(1)} %copy-done.6, f32[64,256]{1,0:T(8,128)S(1)} %copy-done.5, bf16[768,256]{1,0:T(8,128)(2,1)S(1)} %copy-done, bf16[256,256]{1,0:T(8,128)(2,1)S(1)} %copy-done.4, bf16[64,128]{1,0:T(8,128)(2,1)S(1)} %copy-done.7), custom_call_target="tpu_custom_call" | custom-call | tf_op jit(solution)/shard_map/core/pallas_call | solution.py:237
  34.4 24.3 %all_to_all.22 = bf16[64,7,2,128]{3,2,1,0:T(2,128)(2,1)S(1)} all-to-all(bf16[64,7,2,128]{3,2,1,0:T(2,128)(2,1)S(1)} %bitcast.9), channel_id=1, replica_groups={{280,272,264,256,248,240,232,224,216,208,200,192,184,176,168,160,152,14..., dimensions={0} | all-to-all | bytes 458752 | tf_op jit(solution)/shard_map/all_to_all | solution.py:225
  58.7 0.0 copy-start.1
  58.7 0.0 copy-start.2
  58.7 0.0 copy-start.3
  58.7 0.1 taps.3
  58.8 10.3 %all_to_all.23 = bf16[8,16,128]{2,1,0:T(8,128)(2,1)S(1)} all-to-all(bf16[8,16,128]{2,1,0:T(8,128)(2,1)S(1)} %bitcast.12), channel_id=1, replica_groups={{6,7,0,1,2,3,4,5},{14,15,8,9,10,11,12,13},{22,23,16,17,18,19,20,21},{30..., dimensions={0} | all-to-all | bytes 65536 | tf_op jit(solution)/shard_map/all_to_all | solution.py:253
  69.1 0.0 copy-done.1
  69.1 0.0 copy-done.2
  69.1 0.0 copy-done.3
  69.1 0.9 %grads.1 = (bf16[128,384]{1,0:T(8,128)(2,1)}, bf16[128,384]{1,0:T(8,128)(2,1)}, bf16[128,384]{1,0:T(8,128)(2,1)}, f32[16,128]{1,0:T(8,128)}) custom-call(bf16[896,128]{1,0:T(8,128)(2,1)S(1)} %bitcast.7, bf16[128,128]{1,0:T(8,128)(2,1)S(1)} %bitcast.11, bf16[128,384]{1,0:T(8,128)(2,1)S(1)} %copy-done.3, bf16[128,384]{1,0:T(8,128)(2,1)S(1)} %copy-done.2, ...), custom_call_target="tpu_custom_call" | custom-call | tf_op jit(solution)/shard_map/grads/pallas_call | solution.py:254
Async XLA Ops:
  0.6 32.5 %copy-start.4 = (bf16[256,256]{1,0:T(8,128)(2,1)S(1)}, bf16[256,256]{1,0:T(8,128)(2,1)}, u32[]{:S(2)}) copy-start(bf16[256,256]{1,0:T(8,128)(2,1)} %constant.13.clone.ib) | copy-start | bytes 393220
  0.6 32.5 %copy-start.6 = (bf16[128,128]{1,0:T(8,128)(2,1)S(1)}, bf16[128,128]{1,0:T(8,128)(2,1)}, u32[]{:S(2)}) copy-start(bf16[128,128]{1,0:T(8,128)(2,1)} %constant.10.clone.fa) | copy-start | bytes 98308
  0.7 32.5 %copy-start.7 = (bf16[64,128]{1,0:T(8,128)(2,1)S(1)}, bf16[64,128]{1,0:T(8,128)(2,1)}, u32[]{:S(2)}) copy-start(bf16[64,128]{1,0:T(8,128)(2,1)} %constant.14.clone.ia) | copy-start | bytes 49156
  2.1 31.1 %copy-start = (bf16[768,256]{1,0:T(8,128)(2,1)S(1)}, bf16[768,256]{1,0:T(8,128)(2,1)}, u32[]{:S(2)}) copy-start(bf16[768,256]{1,0:T(8,128)(2,1)} %constant.12.clone.fb) | copy-start | bytes 1179652
  2.1 31.1 %copy-start.5 = (f32[64,256]{1,0:T(8,128)S(1)}, f32[64,256]{1,0:T(8,128)}, u32[]{:S(2)}) copy-start(f32[64,256]{1,0:T(8,128)} %constant.11.clone.tw) | copy-start | bytes 196612
  58.7 10.5 %copy-start.1 = (bf16[128,384]{1,0:T(8,128)(2,1)S(1)}, bf16[128,384]{1,0:T(8,128)(2,1)}, u32[]{:S(2)}) copy-start(bf16[128,384]{1,0:T(8,128)(2,1)} %key_in.3) | copy-start | bytes 294916
  58.7 10.5 %copy-start.2 = (bf16[128,384]{1,0:T(8,128)(2,1)S(1)}, bf16[128,384]{1,0:T(8,128)(2,1)}, u32[]{:S(2)}) copy-start(bf16[128,384]{1,0:T(8,128)(2,1)} %value.3) | copy-start | bytes 294916
  58.7 10.5 %copy-start.3 = (bf16[128,384]{1,0:T(8,128)(2,1)S(1)}, bf16[128,384]{1,0:T(8,128)(2,1)}, u32[]{:S(2)}) copy-start(bf16[128,384]{1,0:T(8,128)(2,1)} %cot.1) | copy-start | bytes 294916

commit v10 on v7

--- a/solution.py
+++ b/solution.py
@@ -197,7 +197,7 @@
     fils = filters // blocks
     per = (2 * repeat + 1) * fils
     scale = 1.0 / (length * math.sqrt(length))
-    first = blocks // 2 + 3
+    first = blocks // 2 + 7
     group = [(3 * groups // 4 + c) % groups for c in range(groups)]
     order = [(first - i) % blocks for i in range(blocks)]
     tables = [jnp.asarray(t) for t in make_tables(blocks, width, order)]

time: 70.8 us -> 70.9 us (level)
  no operation moved by 1% of the time
where the time goes in v10:
time: 70.9 us; the launch traced here: 70 us
  blocking collectives  65.7 us (93%)
  Pallas kernels  3.53 us (5%)
  between operations  0.72 us (1%)
    all_to_all x2, blocking collectives, swap(): lax.all_to_all(array.reshape(shape), 'seq', split_axis=0, concat_axis=0,...  55.4 us
    all_to_all x1, blocking collectives, local(): lax.all_to_all(taps, 'chan', split_axis=0, concat_axis=0, tiled=True, axi...  10.3 us

profile of v10, /device:TPU:6, one launch (start us, length us, event | category | flops | bytes accessed | tf_op | source)
XLA Modules:
  0.0 70.0 jit_solution(6785291615621495536)
XLA Ops:
  0.6 0.0 copy-start.4
  0.6 0.0 copy-start.6
  0.7 0.0 copy-start.7
  0.7 1.4 %gate.1 = bf16[896,128]{1,0:T(8,128)(2,1)S(1)} custom-call(bf16[128,384]{1,0:T(8,128)(2,1)} %query.1, bf16[128,384]{1,0:T(8,128)(2,1)} %key_in.3, bf16[128,384]{1,0:T(8,128)(2,1)} %value.3, bf16[128,384]{1,0:T(8,128)(2,1)} %cot.1, bf16[128,128]{1,0:T(8,128)(2,1)} %taps.2), custom_call_target="tpu_custom_call" | custom-call | tf_op jit(solution)/shard_map/gate/pallas_call | solution.py:214
  2.1 0.0 copy-start
  2.1 0.0 copy-start.5
  2.1 31.0 %all_to_all.21 = bf16[64,7,2,128]{3,2,1,0:T(2,128)(2,1)S(1)} all-to-all(bf16[64,7,2,128]{3,2,1,0:T(2,128)(2,1)S(1)} %bitcast.10), channel_id=1, replica_groups={{312,304,296,288,280,272,264,256,248,240,232,224,216,208,200,192,184,17..., dimensions={0} | all-to-all | bytes 458752 | tf_op jit(solution)/shard_map/all_to_all | solution.py:210
  33.1 0.0 copy-done.4
  33.1 0.0 copy-done.6
  33.1 0.0 copy-done.7
  33.1 0.0 copy-done
  33.1 0.0 copy-done.5
  33.1 1.2 %core.1 = bf16[896,128]{1,0:T(8,128)(2,1)S(1)} custom-call(bf16[896,128]{1,0:T(8,128)(2,1)S(1)} %bitcast.8, bf16[128,128]{1,0:T(8,128)(2,1)S(1)} %copy-done.6, f32[64,256]{1,0:T(8,128)S(1)} %copy-done.5, bf16[768,256]{1,0:T(8,128)(2,1)S(1)} %copy-done, bf16[256,256]{1,0:T(8,128)(2,1)S(1)} %copy-done.4, bf16[64,128]{1,0:T(8,128)(2,1)S(1)} %copy-done.7), custom_call_target="tpu_custom_call" | custom-call | tf_op jit(solution)/shard_map/core/pallas_call | solution.py:222
  34.3 24.3 %all_to_all.22 = bf16[64,7,2,128]{3,2,1,0:T(2,128)(2,1)S(1)} all-to-all(bf16[64,7,2,128]{3,2,1,0:T(2,128)(2,1)S(1)} %bitcast.9), channel_id=1, replica_groups={{312,304,296,288,280,272,264,256,248,240,232,224,216,208,200,192,184,17..., dimensions={0} | all-to-all | bytes 458752 | tf_op jit(solution)/shard_map/all_to_all | solution.py:210
  58.6 0.0 copy-start.1
  58.7 0.0 copy-start.2
  58.7 0.0 copy-start.3
  58.7 0.1 taps.3
  58.8 10.3 %all_to_all.23 = bf16[8,16,128]{2,1,0:T(8,128)(2,1)S(1)} all-to-all(bf16[8,16,128]{2,1,0:T(8,128)(2,1)S(1)} %bitcast.12), channel_id=1, replica_groups={{6,7,0,1,2,3,4,5},{14,15,8,9,10,11,12,13},{22,23,16,17,18,19,20,21},{30..., dimensions={0} | all-to-all | bytes 65536 | tf_op jit(solution)/shard_map/all_to_all | solution.py:238
  69.1 0.0 copy-done.1
  69.1 0.0 copy-done.2
  69.1 0.0 copy-done.3
  69.1 0.9 %grads.1 = (bf16[128,384]{1,0:T(8,128)(2,1)}, bf16[128,384]{1,0:T(8,128)(2,1)}, bf16[128,384]{1,0:T(8,128)(2,1)}, f32[16,128]{1,0:T(8,128)}) custom-call(bf16[896,128]{1,0:T(8,128)(2,1)S(1)} %bitcast.7, bf16[128,128]{1,0:T(8,128)(2,1)S(1)} %bitcast.11, bf16[128,384]{1,0:T(8,128)(2,1)S(1)} %copy-done.3, bf16[128,384]{1,0:T(8,128)(2,1)S(1)} %copy-done.2, ...), custom_call_target="tpu_custom_call" | custom-call | tf_op jit(solution)/shard_map/grads/pallas_call | solution.py:239
Async XLA Ops:
  0.6 32.5 %copy-start.4 = (bf16[256,256]{1,0:T(8,128)(2,1)S(1)}, bf16[256,256]{1,0:T(8,128)(2,1)}, u32[]{:S(2)}) copy-start(bf16[256,256]{1,0:T(8,128)(2,1)} %constant.13.clone.ib) | copy-start | bytes 393220
  0.6 32.5 %copy-start.6 = (bf16[128,128]{1,0:T(8,128)(2,1)S(1)}, bf16[128,128]{1,0:T(8,128)(2,1)}, u32[]{:S(2)}) copy-start(bf16[128,128]{1,0:T(8,128)(2,1)} %constant.10.clone.fa) | copy-start | bytes 98308
  0.7 32.5 %copy-start.7 = (bf16[64,128]{1,0:T(8,128)(2,1)S(1)}, bf16[64,128]{1,0:T(8,128)(2,1)}, u32[]{:S(2)}) copy-start(bf16[64,128]{1,0:T(8,128)(2,1)} %constant.14.clone.ia) | copy-start | bytes 49156
  2.1 31.1 %copy-start = (bf16[768,256]{1,0:T(8,128)(2,1)S(1)}, bf16[768,256]{1,0:T(8,128)(2,1)}, u32[]{:S(2)}) copy-start(bf16[768,256]{1,0:T(8,128)(2,1)} %constant.12.clone.fb) | copy-start | bytes 1179652
  2.1 31.1 %copy-start.5 = (f32[64,256]{1,0:T(8,128)S(1)}, f32[64,256]{1,0:T(8,128)}, u32[]{:S(2)}) copy-start(f32[64,256]{1,0:T(8,128)} %constant.11.clone.tw) | copy-start | bytes 196612
  58.6 10.5 %copy-start.1 = (bf16[128,384]{1,0:T(8,128)(2,1)S(1)}, bf16[128,384]{1,0:T(8,128)(2,1)}, u32[]{:S(2)}) copy-start(bf16[128,384]{1,0:T(8,128)(2,1)} %key_in.3) | copy-start | bytes 294916
  58.7 10.5 %copy-start.2 = (bf16[128,384]{1,0:T(8,128)(2,1)S(1)}, bf16[128,384]{1,0:T(8,128)(2,1)}, u32[]{:S(2)}) copy-start(bf16[128,384]{1,0:T(8,128)(2,1)} %value.3) | copy-start | bytes 294916
  58.7 10.5 %copy-start.3 = (bf16[128,384]{1,0:T(8,128)(2,1)S(1)}, bf16[128,384]{1,0:T(8,128)(2,1)}, u32[]{:S(2)}) copy-start(bf16[128,384]{1,0:T(8,128)(2,1)} %cot.1) | copy-start | bytes 294916
